TPU v7x, 512 devices: a whole 4x4x16 slice. The times are simulated.
512 devices in a mesh: seq: 64 (over z, y), head: 8 (over x, core).
Axes of the slice: x: 4, y: 4, z: 16, core: 2. Of those that a mesh axis runs over, the one named last changes fastest.
Arguments:
- queries: bfloat16 [16384, 8192], P(('seq', 'head')), may hold values from -6 to 6
- keys: bfloat16 [16384, 8192], P(('seq', 'head')), may hold values from -6 to 6
- values: bfloat16 [16384, 8192], P(('seq', 'head')), may hold values from -6 to 6
- landmarks: bfloat16 [256, 8192], P('seq', 'head'), may hold values from -6 to 6
- grad_out: bfloat16 [16384, 8192], P(('seq', 'head')), may hold values from -6 to 6
- selections: int32 [256, 16], P('seq'), may hold values from -1 to 255, as said below
Outputs:
- attended: bfloat16 [16384, 8192], P('seq', 'head')
- grad_queries: bfloat16 [16384, 8192], P('seq', 'head')
- grad_keys: bfloat16 [16384, 8192], P('seq', 'head')
- grad_values: bfloat16 [16384, 8192], P('seq', 'head')
- grad_landmarks: bfloat16 [256, 8192], P('seq', 'head')
Inputs may be any that keep to these rules, and one draw needn't show every extreme that they name: `selections`: entry 0 of query block b's list is b. The other live entries are distinct blocks b - o with 1 <= o <= 16; live entries come first and -1 fills the rest. The list of the last block is full.
All inputs are finite; a program needn't handle non-finite values.
Results may differ from a plain program's by a relative error of at most 0.017.
Values may be sent and summed in bfloat16 or wider, within the bound.
A program may use at most 128 MiB of HBM per device.

v0:
```python
from functools import partial

import jax
import jax.numpy as jnp
from jax import lax
from jax.sharding import PartitionSpec as P

HD = 128
BLOCK = 64
REACH = 4


def passed_along(value, axis, by):
    devices = lax.axis_size(axis)
    pairs = [(i, i + by) for i in range(devices) if 0 <= i + by < devices]
    return lax.ppermute(value, axis, pairs)


def attend_picked(
    query_blk, key_sel, value_sel, mark_sel, slot_index, slot_live, own_slot, head_count
):
    block_len = query_blk.shape[0]
    head_dim = query_blk.shape[1] // head_count
    pick_count = slot_index.shape[0]
    scale_q = head_dim ** (-0.5)
    query_heads = query_blk.astype(jnp.bfloat16).reshape(block_len, head_count, head_dim)
    key_heads = key_sel.astype(jnp.bfloat16).reshape(pick_count, block_len, head_count, head_dim)
    value_heads = value_sel.astype(jnp.bfloat16).reshape(
        pick_count, block_len, head_count, head_dim
    )
    mark_heads = mark_sel.astype(jnp.bfloat16).reshape(pick_count, head_count, head_dim)
    scores = (
        jnp.einsum("ihd,ejhd->heij", query_heads, key_heads, preferred_element_type=jnp.float32)
        * scale_q
    )
    row_pos = jnp.arange(block_len)[:, None]
    col_pos = jnp.arange(block_len)[None, :]
    masked = (slot_index == own_slot)[:, None, None] & (col_pos > row_pos)[None, :, :]
    scores = jnp.where(masked[None], -1e30, scores)
    inner_w = jax.nn.softmax(scores, axis=-1)
    coarse = (
        jnp.einsum("ihd,ehd->hie", query_heads, mark_heads, preferred_element_type=jnp.float32)
        * scale_q
    )
    coarse = jnp.where(slot_live[None, None, :], coarse, -1e30)
    gate_w = jax.nn.softmax(coarse, axis=-1)
    weights = (inner_w * jnp.transpose(gate_w, (0, 2, 1))[:, :, :, None]).astype(jnp.bfloat16)
    result = jnp.einsum("heij,ejhd->ihd", weights, value_heads, preferred_element_type=jnp.float32)
    return result.reshape(block_len, head_count * head_dim)


def add_three(first, second):
    return (first[0] + second[0], first[1] + second[1], first[2] + second[2])


def per_device(queries, keys, values, landmarks, grad_out, selections):
    query_rows, key_rows, value_rows, grad_rows = (
        lax.all_to_all(queries, "head", split_axis=1, concat_axis=0, tiled=True),
        lax.all_to_all(keys, "head", split_axis=1, concat_axis=0, tiled=True),
        lax.all_to_all(values, "head", split_axis=1, concat_axis=0, tiled=True),
        lax.all_to_all(grad_out, "head", split_axis=1, concat_axis=0, tiled=True),
    )
    features = query_rows.shape[1]
    row_count = query_rows.shape[0]
    blocks_dev = row_count // BLOCK
    head_count = features // HD
    own_pack = (key_rows, value_rows, landmarks)
    fetched = []
    for distance in range(1, REACH + 1):
        fetched.append(passed_along((own_pack[0], own_pack[1], own_pack[2]), "seq", distance))
    ordered = fetched[::-1] + [own_pack]
    key_win = jnp.concatenate([piece[0] for piece in ordered], axis=0).reshape(-1, BLOCK, features)
    value_win = jnp.concatenate([piece[1] for piece in ordered], axis=0).reshape(
        -1, BLOCK, features
    )
    mark_win = jnp.concatenate([piece[2] for piece in ordered], axis=0)
    window_blocks = mark_win.shape[0]
    shard_pos = lax.axis_index("seq")
    first_block = (shard_pos - REACH) * blocks_dev
    own_slot = REACH * blocks_dev + jnp.arange(blocks_dev)
    slot_live = selections >= 0
    slot_index = jnp.where(slot_live, selections - first_block, own_slot[:, None])
    local_fn = partial(attend_picked, head_count=head_count)

    def per_block(totals, pieces):
        query_blk, grad_blk, index_row, live_row, own_one = pieces
        key_sel = jnp.take(key_win, index_row, axis=0).astype(jnp.float32)
        value_sel = jnp.take(value_win, index_row, axis=0).astype(jnp.float32)
        mark_sel = jnp.take(mark_win, index_row, axis=0).astype(jnp.float32)

        def local(query_f, key_f, value_f, mark_f):
            return local_fn(query_f, key_f, value_f, mark_f, index_row, live_row, own_one)

        result, pull = jax.vjp(local, query_blk.astype(jnp.float32), key_sel, value_sel, mark_sel)
        grad_qb, grad_kb, grad_vb, grad_mb = pull(grad_blk.astype(jnp.float32))
        totals = (
            totals[0].at[index_row].add(grad_kb),
            totals[1].at[index_row].add(grad_vb),
            totals[2].at[index_row].add(grad_mb),
        )
        return (totals, (result.astype(jnp.bfloat16), grad_qb.astype(jnp.bfloat16)))

    start = (
        jnp.zeros((window_blocks, BLOCK, features), jnp.float32),
        jnp.zeros((window_blocks, BLOCK, features), jnp.float32),
        jnp.zeros((window_blocks, features), jnp.float32),
    )
    query_blocks = query_rows.reshape(blocks_dev, BLOCK, features)
    grad_blocks = grad_rows.reshape(blocks_dev, BLOCK, features)
    sums, outputs = lax.scan(
        per_block, start, (query_blocks, grad_blocks, slot_index, slot_live, own_slot)
    )
    attended = outputs[0].reshape(row_count, features)
    grad_q = outputs[1].reshape(row_count, features)
    grad_kwin = sums[0].reshape(REACH + 1, row_count, features)
    grad_vwin = sums[1].reshape(REACH + 1, row_count, features)
    grad_mwin = sums[2].reshape(REACH + 1, blocks_dev, features)

    def grad_part(position):
        return (grad_kwin[position], grad_vwin[position], grad_mwin[position])

    totals = grad_part(REACH)
    for distance in range(1, REACH + 1):
        arrived = passed_along(grad_part(REACH - distance), "seq", -distance)
        totals = add_three(totals, arrived)
    return (
        attended,
        grad_q,
        totals[0].astype(jnp.bfloat16),
        totals[1].astype(jnp.bfloat16),
        totals[2].astype(jnp.bfloat16),
    )


def solution(mesh):
    in_specs = (
        P(("seq", "head"), None),
        P(("seq", "head"), None),
        P(("seq", "head"), None),
        P("seq", "head"),
        P(("seq", "head"), None),
        P("seq", None),
    )
    out_specs = (
        P("seq", "head"),
        P("seq", "head"),
        P("seq", "head"),
        P("seq", "head"),
        P("seq", "head"),
    )
    return jax.shard_map(
        per_device, mesh=mesh, in_specs=in_specs, out_specs=out_specs, check_vma=False
    )
```

profile of v0, /device:TPU:1, one launch (start us, length us, event | category | flops | bytes accessed | tf_op | source)
XLA Modules:
  0.0 614.7 jit_solution(8569496532969502642)
XLA Ops:
  2.6 10.3 %all-to-all-start.3 = ((bf16[32,8,1024]{2,0,1:T(8,128)(2,1)}), bf16[32,8,1024]{2,0,1:T(8,128)(2,1)S(1)}, u32[]{:S(2)}, u32[]{:S(2)}) async-start(bf16[32,8,1024]{2,0,1:T(8,128)(2,1)} %bitcast.232), calls=%async_computation.3 | async-start | bytes 1048576 | tf_op jit(solution)/shard_map/all_to_all | solution.py:59
  22.7 5.6 all-to-all-start.1
  35.3 6.9 %collective-permute-start.9 = (bf16[256,1024]{1,0:T(8,128)(2,1)S(1)}, bf16[256,1024]{1,0:T(8,128)(2,1)}, u32[]{:S(2)}, u32[]{:S(2)}) collective-permute-start(bf16[256,1024]{1,0:T(8,128)(2,1)S(1)} %bitcast.343), channel_id=1, source_target_pairs={{0,24},{8,32},{16,40},{24,48},{32,56},{40,64},{48,72},{56,80},{64,... | collective-permute-start | bytes 1572872 | tf_op jit(solution)/shard_map/ppermute | solution.py:16
  48.6 6.2 %all-to-all-start.2 = ((bf16[32,8,1024]{2,0,1:T(8,128)(2,1)}), bf16[32,8,1024]{2,0,1:T(8,128)(2,1)S(1)}, u32[]{:S(2)}, u32[]{:S(2)}) async-start(bf16[32,8,1024]{2,0,1:T(8,128)(2,1)} %bitcast.233), calls=%async_computation.2 | async-start | bytes 1048576 | tf_op jit(solution)/shard_map/all_to_all | solution.py:58
  58.5 21.6 %collective-permute-start = (bf16[256,1024]{1,0:T(8,128)(2,1)}, bf16[256,1024]{1,0:T(8,128)(2,1)S(1)}, u32[]{:S(2)}, u32[]{:S(2)}) collective-permute-start(bf16[256,1024]{1,0:T(8,128)(2,1)} %bitcast.32), channel_id=1, source_target_pairs={{0,32},{8,40},{16,48},{24,56},{32,64},{40,72},{48,80},{56,88},{64,... | collective-permute-start | bytes 1572872 | tf_op jit(solution)/shard_map/ppermute | solution.py:16
  80.2 6.5 %collective-permute-start.1 = (bf16[256,1024]{1,0:T(8,128)(2,1)}, bf16[256,1024]{1,0:T(8,128)(2,1)}, u32[]{:S(2)}, u32[]{:S(2)}) collective-permute-start(bf16[256,1024]{1,0:T(8,128)(2,1)} %bitcast.32), channel_id=1, source_target_pairs={{0,24},{8,32},{16,40},{24,48},{32,56},{40,64},{48,72},{56,80},{64,... | collective-permute-start | bytes 1572872 | tf_op jit(solution)/shard_map/ppermute | solution.py:16
  92.6 5.7 all-to-all-start
  98.3 9.9 %collective-permute-done.1 = bf16[256,1024]{1,0:T(8,128)(2,1)} collective-permute-done((bf16[256,1024]{1,0:T(8,128)(2,1)}, bf16[256,1024]{1,0:T(8,128)(2,1)}, u32[]{:S(2)}, u32[]{:S(2)}) %collective-permute-start.1) | collective-permute-done | bytes 524320 | tf_op jit(solution)/shard_map/ppermute | solution.py:16
  119.2 225.4 %while.18 = (s32[]{:T(128)}, f32[20,64,1024]{2,1,0:T(8,128)}, f32[20,64,1024]{2,1,0:T(8,128)}, f32[20,1024]{1,0:T(8,128)}, bf16[4,64,1024]{2,1,0:T(8,128)(2,1)},...) while((s32[]{:T(128)}, f32[20,64,1024]{2,1,0:T(8,128)}, ...), condition=%wide.region_11.13_spmd, body=%wide.region_0.12_spmd.sunk | while | flops 842108032 | bytes 162792816 | solution.py:110
  135.2 3.9 fusion.127
  140.8 5.9 fusion.132
  153.7 9.2 %scatter_fusion = f32[20,64,1024]{2,1,0:T(8,128)} fusion(f32[20,64,1024]{2,1,0:T(8,128)} %get-tuple-element.289, s32[16]{0:T(128)S(1)} %fusion.123, f32[16,64,1024]{2,1,0:T(8,128)} %bitcast.328), kind=kCustom, calls=%fused_computation.3.clone.1 | custom fusion | flops 1048576 | bytes 12582976 | tf_op jit(solution)/shard_map/while/body/eval_jaxpr/scatter-add | solution.py:97
  166.2 9.0 %scatter_fusion.1 = f32[20,64,1024]{2,1,0:T(8,128)} fusion(f32[20,64,1024]{2,1,0:T(8,128)} %get-tuple-element.290, s32[16]{0:T(128)S(1)} %fusion.123, f32[16,64,1024]{2,1,0:T(8,128)} %copy_bitcast_fusion.11), kind=kCustom, calls=%fused_computation.4.clone.1 | custom fusion | flops 1048576 | bytes 12582976 | tf_op jit(solution)/shard_map/while/body/eval_jaxpr/scatter-add | solution.py:98
  191.2 3.9 fusion.127
  196.8 5.9 fusion.132
  209.7 9.2 %scatter_fusion = f32[20,64,1024]{2,1,0:T(8,128)} fusion(f32[20,64,1024]{2,1,0:T(8,128)} %get-tuple-element.289, s32[16]{0:T(128)S(1)} %fusion.123, f32[16,64,1024]{2,1,0:T(8,128)} %bitcast.328), kind=kCustom, calls=%fused_computation.3.clone.1 | custom fusion | flops 1048576 | bytes 12582976 | tf_op jit(solution)/shard_map/while/body/eval_jaxpr/scatter-add | solution.py:97
  222.2 9.2 %scatter_fusion.1 = f32[20,64,1024]{2,1,0:T(8,128)} fusion(f32[20,64,1024]{2,1,0:T(8,128)} %get-tuple-element.290, s32[16]{0:T(128)S(1)} %fusion.123, f32[16,64,1024]{2,1,0:T(8,128)} %copy_bitcast_fusion.11), kind=kCustom, calls=%fused_computation.4.clone.1 | custom fusion | flops 1048576 | bytes 12582976 | tf_op jit(solution)/shard_map/while/body/eval_jaxpr/scatter-add | solution.py:98
  253.0 5.9 fusion.132
  265.9 9.1 %scatter_fusion = f32[20,64,1024]{2,1,0:T(8,128)} fusion(f32[20,64,1024]{2,1,0:T(8,128)} %get-tuple-element.289, s32[16]{0:T(128)S(1)} %fusion.123, f32[16,64,1024]{2,1,0:T(8,128)} %bitcast.328), kind=kCustom, calls=%fused_computation.3.clone.1 | custom fusion | flops 1048576 | bytes 12582976 | tf_op jit(solution)/shard_map/while/body/eval_jaxpr/scatter-add | solution.py:97
  278.3 9.2 %scatter_fusion.1 = f32[20,64,1024]{2,1,0:T(8,128)} fusion(f32[20,64,1024]{2,1,0:T(8,128)} %get-tuple-element.290, s32[16]{0:T(128)S(1)} %fusion.123, f32[16,64,1024]{2,1,0:T(8,128)} %copy_bitcast_fusion.11), kind=kCustom, calls=%fused_computation.4.clone.1 | custom fusion | flops 1048576 | bytes 12582976 | tf_op jit(solution)/shard_map/while/body/eval_jaxpr/scatter-add | solution.py:98
  303.5 3.9 fusion.127
  309.1 5.9 fusion.132
  322.0 9.5 %scatter_fusion = f32[20,64,1024]{2,1,0:T(8,128)} fusion(f32[20,64,1024]{2,1,0:T(8,128)} %get-tuple-element.289, s32[16]{0:T(128)S(1)} %fusion.123, f32[16,64,1024]{2,1,0:T(8,128)} %bitcast.328), kind=kCustom, calls=%fused_computation.3.clone.1 | custom fusion | flops 1048576 | bytes 12582976 | tf_op jit(solution)/shard_map/while/body/eval_jaxpr/scatter-add | solution.py:97
  334.9 9.7 %scatter_fusion.1 = f32[20,64,1024]{2,1,0:T(8,128)} fusion(f32[20,64,1024]{2,1,0:T(8,128)} %get-tuple-element.290, s32[16]{0:T(128)S(1)} %fusion.123, f32[16,64,1024]{2,1,0:T(8,128)} %copy_bitcast_fusion.11), kind=kCustom, calls=%fused_computation.4.clone.1 | custom fusion | flops 1048576 | bytes 12582976 | tf_op jit(solution)/shard_map/while/body/eval_jaxpr/scatter-add | solution.py:98
  344.6 5.2 fusion.73
  356.3 22.9 %collective-permute-done.20 = f32[4,1024]{1,0:T(4,128)S(1)} collective-permute-done((f32[4,1024]{1,0:T(4,128)S(1)}, f32[4,1024]{1,0:T(4,128)S(1)}, u32[]{:S(2)}, u32[]{:S(2)}) %collective-permute-start.20) | collective-permute-done | bytes 16416 | tf_op jit(solution)/shard_map/ppermute | solution.py:16
  380.4 95.8 %collective-permute-done.23 = f32[4,1024]{1,0:T(4,128)S(1)} collective-permute-done((f32[4,1024]{1,0:T(4,128)S(1)}, f32[4,1024]{1,0:T(4,128)S(1)}, u32[]{:S(2)}, u32[]{:S(2)}) %collective-permute-start.23) | collective-permute-done | bytes 16416 | tf_op jit(solution)/shard_map/ppermute | solution.py:16
  477.6 7.4 %collective-permute-done.22 = f32[4,1024]{1,0:T(4,128)S(1)} collective-permute-done((f32[4,1024]{1,0:T(4,128)S(1)}, f32[4,1024]{1,0:T(4,128)S(1)}, u32[]{:S(2)}, u32[]{:S(2)}) %collective-permute-start.22) | collective-permute-done | bytes 16416 | tf_op jit(solution)/shard_map/ppermute | solution.py:16
  486.2 4.7 collective-permute-done.21
  498.1 31.2 %collective-permute-done.12 = f32[256,1024]{1,0:T(8,128)S(1)} collective-permute-done((f32[256,1024]{1,0:T(8,128)S(1)}, f32[256,1024]{1,0:T(8,128)S(1)}, u32[]{:S(2)}, u32[]{:S(2)}) %collective-permute-start.12) | collective-permute-done | bytes 1048608 | tf_op jit(solution)/shard_map/ppermute | solution.py:16
  529.2 8.9 %collective-permute-done.13 = f32[256,1024]{1,0:T(8,128)S(1)} collective-permute-done((f32[256,1024]{1,0:T(8,128)S(1)}, f32[256,1024]{1,0:T(8,128)S(1)}, u32[]{:S(2)}, u32[]{:S(2)}) %collective-permute-start.13) | collective-permute-done | bytes 1048608 | tf_op jit(solution)/shard_map/ppermute | solution.py:16
  538.1 75.2 %collective-permute-done.15 = f32[256,1024]{1,0:T(8,128)S(1)} collective-permute-done((f32[256,1024]{1,0:T(8,128)S(1)}, f32[256,1024]{1,0:T(8,128)S(1)}, u32[]{:S(2)}, u32[]{:S(2)}) %collective-permute-start.15) | collective-permute-done | bytes 1048608 | tf_op jit(solution)/shard_map/ppermute | solution.py:16
  (333 shorter events, 179.2 us)
Async XLA Ops:
  0.6 41.7 %copy-start.16 = (bf16[4,1024]{1,0:T(4,128)(2,1)S(1)}, bf16[4,1024]{1,0:T(4,128)(2,1)}, u32[]{:S(2)}) copy-start(bf16[4,1024]{1,0:T(4,128)(2,1)} %param.13) | copy-start | bytes 24580
  0.6 41.6 %copy-start.15 = (s32[4,16]{1,0:T(4,128)S(1)}, s32[4,16]{1,0:T(4,128)}, u32[]{:S(2)}) copy-start(s32[4,16]{1,0:T(4,128)} %param.15) | copy-start | bytes 772
  0.7 46.2 %copy-start.10 = (bf16[32,8192]{1,0:T(8,128)(2,1)S(1)}, bf16[32,8192]{1,0:T(8,128)(2,1)}, u32[]{:S(2)}) copy-start(bf16[32,8192]{1,0:T(8,128)(2,1)} %param.10) | copy-start | bytes 1572868
  0.7 47.1 %copy-start.11 = (bf16[32,8192]{1,0:T(8,128)(2,1)S(1)}, bf16[32,8192]{1,0:T(8,128)(2,1)}, u32[]{:S(2)}) copy-start(bf16[32,8192]{1,0:T(8,128)(2,1)} %param.14) | copy-start | bytes 1572868
  2.6 20.1 %all-to-all-start.3 = ((bf16[32,8,1024]{2,0,1:T(8,128)(2,1)}), bf16[32,8,1024]{2,0,1:T(8,128)(2,1)S(1)}, u32[]{:S(2)}, u32[]{:S(2)}) async-start(bf16[32,8,1024]{2,0,1:T(8,128)(2,1)} %bitcast.232), calls=%async_computation.3 | async-start | bytes 1048576 | tf_op jit(solution)/shard_map/all_to_all | solution.py:59
  12.9 22.4 %collective-permute-start.6 = (bf16[4,1024]{1,0:T(4,128)(2,1)}, bf16[4,1024]{1,0:T(4,128)(2,1)S(1)}, u32[]{:S(2)}, u32[]{:S(2)}) collective-permute-start(bf16[4,1024]{1,0:T(4,128)(2,1)} %param.13), channel_id=1, source_target_pairs={{0,16},{8,24},{16,32},{24,40},{32,48},{40,56},{48,64},{56,72},{64,... | collective-permute-start | bytes 24584 | tf_op jit(solution)/shard_map/ppermute | solution.py:16
  14.2 28.1 %collective-permute-start.5 = (bf16[4,1024]{1,0:T(4,128)(2,1)}, bf16[4,1024]{1,0:T(4,128)(2,1)S(1)}, u32[]{:S(2)}, u32[]{:S(2)}) collective-permute-start(bf16[4,1024]{1,0:T(4,128)(2,1)} %param.13), channel_id=1, source_target_pairs={{0,24},{8,32},{16,40},{24,48},{32,56},{40,64},{48,72},{56,80},{64,... | collective-permute-start | bytes 24584 | tf_op jit(solution)/shard_map/ppermute | solution.py:16
  17.3 26.7 %collective-permute-start.4 = (bf16[4,1024]{1,0:T(4,128)(2,1)}, bf16[4,1024]{1,0:T(4,128)(2,1)S(1)}, u32[]{:S(2)}, u32[]{:S(2)}) collective-permute-start(bf16[4,1024]{1,0:T(4,128)(2,1)} %param.13), channel_id=1, source_target_pairs={{0,32},{8,40},{16,48},{24,56},{32,64},{40,72},{48,80},{56,88},{64,... | collective-permute-start | bytes 24584 | tf_op jit(solution)/shard_map/ppermute | solution.py:16
  22.7 25.9 %all-to-all-start.1 = ((bf16[32,8,1024]{2,0,1:T(8,128)(2,1)}), bf16[32,8,1024]{2,0,1:T(8,128)(2,1)}, u32[]{:S(2)}, u32[]{:S(2)}) async-start(bf16[32,8,1024]{2,0,1:T(8,128)(2,1)} %bitcast.234), calls=%async_computation.1 | async-start | bytes 1048576 | tf_op jit(solution)/shard_map/all_to_all | solution.py:60
  28.4 30.1 %collective-permute-start.8 = (bf16[256,1024]{1,0:T(8,128)(2,1)S(1)}, bf16[256,1024]{1,0:T(8,128)(2,1)S(1)}, u32[]{:S(2)}, u32[]{:S(2)}) collective-permute-start(bf16[256,1024]{1,0:T(8,128)(2,1)S(1)} %bitcast.341), channel_id=1, source_target_pairs={{0,32},{8,40},{16,48},{24,56},{32,64},{40,72},{48,80},{56,88},{64,... | collective-permute-start | bytes 1572872 | tf_op jit(solution)/shard_map/ppermute | solution.py:16
  32.0 55.8 %collective-permute-start.10 = (bf16[256,1024]{1,0:T(8,128)(2,1)S(1)}, bf16[256,1024]{1,0:T(8,128)(2,1)S(1)}, u32[]{:S(2)}, u32[]{:S(2)}) collective-permute-start(bf16[256,1024]{1,0:T(8,128)(2,1)S(1)} %bitcast.342), channel_id=1, source_target_pairs={{0,16},{8,24},{16,32},{24,40},{32,48},{40,56},{48,64},{56,72},{64,... | collective-permute-start | bytes 1572872 | tf_op jit(solution)/shard_map/ppermute | solution.py:16
  35.3 44.8 %collective-permute-start.9 = (bf16[256,1024]{1,0:T(8,128)(2,1)S(1)}, bf16[256,1024]{1,0:T(8,128)(2,1)}, u32[]{:S(2)}, u32[]{:S(2)}) collective-permute-start(bf16[256,1024]{1,0:T(8,128)(2,1)S(1)} %bitcast.343), channel_id=1, source_target_pairs={{0,24},{8,32},{16,40},{24,48},{32,56},{40,64},{48,72},{56,80},{64,... | collective-permute-start | bytes 1572872 | tf_op jit(solution)/shard_map/ppermute | solution.py:16
  42.3 6.2 %collective-permute-start.7 = (bf16[4,1024]{1,0:T(4,128)(2,1)S(1)}, bf16[4,1024]{1,0:T(4,128)(2,1)S(1)}, u32[]{:S(2)}, u32[]{:S(2)}) collective-permute-start(bf16[4,1024]{1,0:T(4,128)(2,1)S(1)} %copy-done.16), channel_id=1, source_target_pairs={{0,8},{8,16},{16,24},{24,32},{32,40},{40,48},{48,56},{56,64},{64,7... | collective-permute-start | bytes 24584 | tf_op jit(solution)/shard_map/ppermute | solution.py:16
  44.0 45.9 %collective-permute-start.11 = (bf16[256,1024]{1,0:T(8,128)(2,1)S(1)}, bf16[256,1024]{1,0:T(8,128)(2,1)}, u32[]{:S(2)}, u32[]{:S(2)}) collective-permute-start(bf16[256,1024]{1,0:T(8,128)(2,1)S(1)} %bitcast.344), channel_id=1, source_target_pairs={{0,8},{8,16},{16,24},{24,32},{32,40},{40,48},{48,56},{56,64},{64,7... | collective-permute-start | bytes 1572872 | tf_op jit(solution)/shard_map/ppermute | solution.py:16
  48.6 44.0 %all-to-all-start.2 = ((bf16[32,8,1024]{2,0,1:T(8,128)(2,1)}), bf16[32,8,1024]{2,0,1:T(8,128)(2,1)S(1)}, u32[]{:S(2)}, u32[]{:S(2)}) async-start(bf16[32,8,1024]{2,0,1:T(8,128)(2,1)} %bitcast.233), calls=%async_computation.2 | async-start | bytes 1048576 | tf_op jit(solution)/shard_map/all_to_all | solution.py:58
  54.9 55.5 %collective-permute-start.3 = (bf16[256,1024]{1,0:T(8,128)(2,1)}, bf16[256,1024]{1,0:T(8,128)(2,1)}, u32[]{:S(2)}, u32[]{:S(2)}) collective-permute-start(bf16[256,1024]{1,0:T(8,128)(2,1)} %bitcast.32), channel_id=1, source_target_pairs={{0,8},{8,16},{16,24},{24,32},{32,40},{40,48},{48,56},{56,64},{64,7... | collective-permute-start | bytes 1572872 | tf_op jit(solution)/shard_map/ppermute | solution.py:16
  58.5 34.0 %collective-permute-start = (bf16[256,1024]{1,0:T(8,128)(2,1)}, bf16[256,1024]{1,0:T(8,128)(2,1)S(1)}, u32[]{:S(2)}, u32[]{:S(2)}) collective-permute-start(bf16[256,1024]{1,0:T(8,128)(2,1)} %bitcast.32), channel_id=1, source_target_pairs={{0,32},{8,40},{16,48},{24,56},{32,64},{40,72},{48,80},{56,88},{64,... | collective-permute-start | bytes 1572872 | tf_op jit(solution)/shard_map/ppermute | solution.py:16
  80.2 28.0 %collective-permute-start.1 = (bf16[256,1024]{1,0:T(8,128)(2,1)}, bf16[256,1024]{1,0:T(8,128)(2,1)}, u32[]{:S(2)}, u32[]{:S(2)}) collective-permute-start(bf16[256,1024]{1,0:T(8,128)(2,1)} %bitcast.32), channel_id=1, source_target_pairs={{0,24},{8,32},{16,40},{24,48},{32,56},{40,64},{48,72},{56,80},{64,... | collective-permute-start | bytes 1572872 | tf_op jit(solution)/shard_map/ppermute | solution.py:16
  87.8 21.5 %collective-permute-start.2 = (bf16[256,1024]{1,0:T(8,128)(2,1)}, bf16[256,1024]{1,0:T(8,128)(2,1)}, u32[]{:S(2)}, u32[]{:S(2)}) collective-permute-start(bf16[256,1024]{1,0:T(8,128)(2,1)} %bitcast.32), channel_id=1, source_target_pairs={{0,16},{8,24},{16,32},{24,40},{32,48},{40,56},{48,64},{56,72},{64,... | collective-permute-start | bytes 1572872 | tf_op jit(solution)/shard_map/ppermute | solution.py:16
  92.6 19.9 %all-to-all-start = ((bf16[32,8,1024]{2,0,1:T(8,128)(2,1)}), bf16[32,8,1024]{2,0,1:T(8,128)(2,1)}, u32[]{:S(2)}, u32[]{:S(2)}) async-start(bf16[32,8,1024]{2,0,1:T(8,128)(2,1)} %bitcast.346), calls=%async_computation | async-start | bytes 1048576 | tf_op jit(solution)/shard_map/all_to_all | solution.py:61
  349.7 142.4 %collective-permute-start.19 = (f32[256,1024]{1,0:T(8,128)S(1)}, f32[256,1024]{1,0:T(8,128)S(1)}, u32[]{:S(2)}, u32[]{:S(2)}) collective-permute-start(f32[256,1024]{1,0:T(8,128)S(1)} %bitcast.354), channel_id=1, source_target_pairs={{32,0},{40,8},{48,16},{56,24},{64,32},{72,40},{80,48},{88,56},{96,... | collective-permute-start | bytes 3145736 | tf_op jit(solution)/shard_map/ppermute | solution.py:16
  351.0 142.5 %collective-permute-start.18 = (f32[256,1024]{1,0:T(8,128)S(1)}, f32[256,1024]{1,0:T(8,128)S(1)}, u32[]{:S(2)}, u32[]{:S(2)}) collective-permute-start(f32[256,1024]{1,0:T(8,128)S(1)} %bitcast.353), channel_id=1, source_target_pairs={{24,0},{32,8},{40,16},{48,24},{56,32},{64,40},{72,48},{80,56},{88,... | collective-permute-start | bytes 3145736 | tf_op jit(solution)/shard_map/ppermute | solution.py:16
  352.3 142.5 %collective-permute-start.17 = (f32[256,1024]{1,0:T(8,128)S(1)}, f32[256,1024]{1,0:T(8,128)S(1)}, u32[]{:S(2)}, u32[]{:S(2)}) collective-permute-start(f32[256,1024]{1,0:T(8,128)S(1)} %bitcast.352), channel_id=1, source_target_pairs={{16,0},{24,8},{32,16},{40,24},{48,32},{56,40},{64,48},{72,56},{80,... | collective-permute-start | bytes 3145736 | tf_op jit(solution)/shard_map/ppermute | solution.py:16
  353.6 143.1 %collective-permute-start.16 = (f32[256,1024]{1,0:T(8,128)S(1)}, f32[256,1024]{1,0:T(8,128)S(1)}, u32[]{:S(2)}, u32[]{:S(2)}) collective-permute-start(f32[256,1024]{1,0:T(8,128)S(1)} %bitcast.351), channel_id=1, source_target_pairs={{8,0},{16,8},{24,16},{32,24},{40,32},{48,40},{56,48},{64,56},{72,6... | collective-permute-start | bytes 3145736 | tf_op jit(solution)/shard_map/ppermute | solution.py:16
  355.0 24.2 %collective-permute-start.20 = (f32[4,1024]{1,0:T(4,128)S(1)}, f32[4,1024]{1,0:T(4,128)S(1)}, u32[]{:S(2)}, u32[]{:S(2)}) collective-permute-start(f32[4,1024]{1,0:T(4,128)S(1)} %get-tuple-element.143), channel_id=1, source_target_pairs={{8,0},{16,8},{24,16},{32,24},{40,32},{48,40},{56,48},{64,56},{72,6... | collective-permute-start | bytes 49160 | tf_op jit(solution)/shard_map/ppermute | solution.py:16
  379.1 97.1 %collective-permute-start.23 = (f32[4,1024]{1,0:T(4,128)S(1)}, f32[4,1024]{1,0:T(4,128)S(1)}, u32[]{:S(2)}, u32[]{:S(2)}) collective-permute-start(f32[4,1024]{1,0:T(4,128)S(1)} %get-tuple-element.144), channel_id=1, source_target_pairs={{32,0},{40,8},{48,16},{56,24},{64,32},{72,40},{80,48},{88,56},{96,... | collective-permute-start | bytes 49160 | tf_op jit(solution)/shard_map/ppermute | solution.py:16
  476.3 8.7 %collective-permute-start.22 = (f32[4,1024]{1,0:T(4,128)S(1)}, f32[4,1024]{1,0:T(4,128)S(1)}, u32[]{:S(2)}, u32[]{:S(2)}) collective-permute-start(f32[4,1024]{1,0:T(4,128)S(1)} %get-tuple-element.145), channel_id=1, source_target_pairs={{24,0},{32,8},{40,16},{48,24},{56,32},{64,40},{72,48},{80,56},{88,... | collective-permute-start | bytes 49160 | tf_op jit(solution)/shard_map/ppermute | solution.py:16
  484.9 6.0 collective-permute-start.21
  490.9 38.3 %collective-permute-start.12 = (f32[256,1024]{1,0:T(8,128)S(1)}, f32[256,1024]{1,0:T(8,128)S(1)}, u32[]{:S(2)}, u32[]{:S(2)}) collective-permute-start(f32[256,1024]{1,0:T(8,128)S(1)} %bitcast.350), channel_id=1, source_target_pairs={{8,0},{16,8},{24,16},{32,24},{40,32},{48,40},{56,48},{64,56},{72,6... | collective-permute-start | bytes 3145736 | tf_op jit(solution)/shard_map/ppermute | solution.py:16
  492.2 45.9 %collective-permute-start.13 = (f32[256,1024]{1,0:T(8,128)S(1)}, f32[256,1024]{1,0:T(8,128)S(1)}, u32[]{:S(2)}, u32[]{:S(2)}) collective-permute-start(f32[256,1024]{1,0:T(8,128)S(1)} %bitcast.349), channel_id=1, source_target_pairs={{16,0},{24,8},{32,16},{40,24},{48,32},{56,40},{64,48},{72,56},{80,... | collective-permute-start | bytes 3145736 | tf_op jit(solution)/shard_map/ppermute | solution.py:16
  493.5 44.6 %collective-permute-start.14 = (f32[256,1024]{1,0:T(8,128)S(1)}, f32[256,1024]{1,0:T(8,128)S(1)}, u32[]{:S(2)}, u32[]{:S(2)}) collective-permute-start(f32[256,1024]{1,0:T(8,128)S(1)} %bitcast.348), channel_id=1, source_target_pairs={{24,0},{32,8},{40,16},{48,24},{56,32},{64,40},{72,48},{80,56},{88,... | collective-permute-start | bytes 3145736 | tf_op jit(solution)/shard_map/ppermute | solution.py:16
  494.8 118.5 %collective-permute-start.15 = (f32[256,1024]{1,0:T(8,128)S(1)}, f32[256,1024]{1,0:T(8,128)S(1)}, u32[]{:S(2)}, u32[]{:S(2)}) collective-permute-start(f32[256,1024]{1,0:T(8,128)S(1)} %bitcast.347), channel_id=1, source_target_pairs={{32,0},{40,8},{48,16},{56,24},{64,32},{72,40},{80,48},{88,56},{96,... | collective-permute-start | bytes 3145736 | tf_op jit(solution)/shard_map/ppermute | solution.py:16
  (46 other events, 245.0 us)
where the time goes:
time: 622 us; the launch traced here: 615 us
  waiting for transfers between devices  256 us (41%)
  other arithmetic  124 us (20%)
  starting transfers between devices  103 us (17%)
  local copies, waits for them, and re-layouts  80.3 us (13%)
  matrix products  48.5 us (8%)
    ppermute x24, waiting for transfers between devices, passed_along(): return lax.ppermute(value, axis, pairs)  256 us
    ppermute x24, starting transfers between devices, passed_along(): return lax.ppermute(value, axis, pairs)  75.6 us
    scatter-add x4, other arithmetic, per_block(): totals[1].at[index_row].add(grad_vb)  37.1 us
    scatter-add x4, other arithmetic, per_block(): totals[0].at[index_row].add(grad_kb)  37 us
    dot_general x12, matrix products, attend_picked(): jnp.einsum('ihd,ejhd->heij', query_heads, key_heads, preferred_element_ty...  36.3 us
    reduce_sum x4, other arithmetic, attend_picked(): inner_w * jnp.transpose(gate_w, (0, 2, 1))[:, :, :, None]  15.5 us
    gather x4, local copies, waits for them, and re-layouts, per_block(): key_sel = jnp.take(key_win, index_row, axis=0).astype(jnp.float32)  15.1 us
  transfers between devices with their start and end apart: 28, of which 8 were waited for; matrix products, arithmetic and copies ran while one was open for 2% of the time, Pallas kernels for 0%

commit v1 on v0

v1 whole, which is shorter than its diff:
```python
import jax
import jax.numpy as jnp
from jax import lax
from jax.experimental import pallas as pl
from jax.experimental.pallas import tpu as pltpu
from jax.sharding import PartitionSpec as P

HD = 128
BLOCK = 64
HPD = 2
CH = 256
CB = CH // BLOCK
SCALE = HD ** (-0.5)
LOG2E = 1.4426950408889634
NT = (((1,), (1,)), ((), ()))
NN = (((1,), (0,)), ((), ()))
TN = (((0,), (0,)), ((), ()))


def dot(a, b, dims):
    return lax.dot_general(a, b, dims, preferred_element_type=jnp.float32)


def rows(c):
    return pl.ds(pl.multiple_of(c * CH, CH), CH)


def lanes(h):
    return slice(h * HD, (h + 1) * HD)


def gate_tile(t, first, q, marks, sel, gates):
    row = lax.broadcasted_iota(jnp.int32, (64, CH), 0)
    sub = row % 8
    block = first + (row // 8) * CB + sub
    block = jnp.where((sub < CB) & (block >= 0), block, -2)
    picks = sel[t]
    live = block == picks[0:1]
    for e in range(1, picks.shape[0]):
        live = live | (block == picks[e:e + 1])
    for h in range(HPD):
        mk = marks[:, :, lanes(h)].reshape(64, HD).astype(jnp.bfloat16)
        coarse = dot(mk, q[rows(t), lanes(h)], NT) * SCALE
        coarse = jnp.where(live, coarse, -1e30)
        top = jnp.max(coarse, axis=0, keepdims=True)
        ex = jnp.exp(coarse - top)
        gates[h, t] = (ex / jnp.sum(ex, axis=0, keepdims=True)).reshape(8, 8, CH)


def cell(t, kc, diag, q, d, k, v, kt, vt, gates, dgates, ot, dqt, dk, dv):
    for h in range(HPD):
        qh = q[rows(t), lanes(h)]
        dh = d[rows(t), lanes(h)]
        s = dot(k[rows(kc), lanes(h)], qh, NT)
        g = dot(v[rows(kc), lanes(h)], dh, NT)
        if diag:
            j = lax.broadcasted_iota(jnp.int32, (CH, CH), 0)
            i = lax.broadcasted_iota(jnp.int32, (CH, CH), 1)
            s = jnp.where(j > i, -1e30, s)
        s = s.reshape(CB, BLOCK, CH)
        g = g.reshape(CB, BLOCK, CH)
        top = jnp.max(s, axis=1, keepdims=True)
        p = jnp.exp2((s - top) * (SCALE * LOG2E))
        rz = 1.0 / jnp.sum(p, axis=1, keepdims=True)
        dg = jnp.sum(p * g, axis=1, keepdims=True) * rz
        gate = gates[h, t, kc][0:CB].reshape(CB, 1, CH)
        w = p * (gate * rz)
        ds = w * (g - dg)
        dgates[h, t, kc, 0:CB] = dg.reshape(CB, CH)
        wb = w.astype(jnp.bfloat16).reshape(CH, CH)
        sb = ds.astype(jnp.bfloat16).reshape(CH, CH)
        ot[h, t] += dot(vt[h, kc], wb, NN)
        dqt[h, t] += dot(kt[h, kc], sb, NN)
        dv[kc, :, lanes(h)] += dot(wb, dh, NN)
        dk[kc, :, lanes(h)] += dot(sb, qh, NN)


def transpose_chunk(kc, src, dst):
    for h in range(HPD):
        dst[h, kc] = src[rows(kc), lanes(h)].T


def close_tile(t, q, marks, gates, dgates, ot, dqt, dm, o_out, dq_out):
    for h in range(HPD):
        gate = gates[h, t].reshape(64, CH)
        dg = dgates[h, t].reshape(64, CH)
        dc = gate * (dg - jnp.sum(gate * dg, axis=0, keepdims=True))
        dcb = dc.astype(jnp.bfloat16)
        mk = marks[:, :, lanes(h)].reshape(64, HD).astype(jnp.bfloat16)
        dq = dqt[h, t] + dot(mk, dcb, TN)
        o_out[rows(t), lanes(h)] = ot[h, t].T.astype(jnp.bfloat16)
        dq_out[rows(t), lanes(h)] = (dq * SCALE).T.astype(jnp.bfloat16)
        dm[:, :, lanes(h)] += (dot(dcb, q[rows(t), lanes(h)], NN) * SCALE).reshape(8, 8, HD)


def all_scratch():
    f = jnp.float32
    return [
        pltpu.VMEM((HPD, 8, HD, CH), jnp.bfloat16),
        pltpu.VMEM((HPD, 8, HD, CH), jnp.bfloat16),
        pltpu.VMEM((HPD, 4, 8, 8, CH), f),
        pltpu.VMEM((HPD, 4, 8, 8, CH), f),
        pltpu.VMEM((HPD, 4, HD, CH), f),
        pltpu.VMEM((HPD, 4, HD, CH), f),
        pltpu.VMEM((8, CH, HPD * HD), f),
        pltpu.VMEM((8, CH, HPD * HD), f),
    ]


def local_kernel(first_ref, q, d, k, v, marks, sel, o_out, dq_out, dk_out, dv_out, dm,
                 kt, vt, gates, dgates, ot, dqt, dk, dv):
    first = first_ref[0]
    ot[...] = jnp.zeros_like(ot)
    dqt[...] = jnp.zeros_like(dqt)
    dk[...] = jnp.zeros_like(dk)
    dv[...] = jnp.zeros_like(dv)
    dgates[...] = jnp.zeros_like(dgates)
    dm[...] = jnp.zeros_like(dm)

    @pl.loop(0, 4)
    def _(t):
        gate_tile(t, first, q, marks, sel, gates)

    @pl.loop(0, 8)
    def _(kc):
        transpose_chunk(kc, k, kt)
        transpose_chunk(kc, v, vt)

    args = (q, d, k, v, kt, vt, gates, dgates, ot, dqt, dk, dv)

    @pl.loop(0, 4)
    def _(t):
        cell(t, t + 4, True, *args)

        @pl.loop(t, t + 4)
        def _(kc):
            cell(t, kc, False, *args)

        close_tile(t, q, marks, gates, dgates, ot, dqt, dm, o_out, dq_out)

    @pl.loop(0, 8)
    def _(kc):
        dk_out[rows(kc), :] = (dk[kc] * SCALE).astype(jnp.bfloat16)
        dv_out[rows(kc), :] = dv[kc].astype(jnp.bfloat16)


def local_call(first, q, d, k, v, marks, sel):
    vm = pl.BlockSpec(memory_space=pltpu.VMEM)
    b = jnp.bfloat16
    return pl.pallas_call(
        local_kernel,
        out_shape=[
            jax.ShapeDtypeStruct((1024, 256), b),
            jax.ShapeDtypeStruct((1024, 256), b),
            jax.ShapeDtypeStruct((2048, 256), b),
            jax.ShapeDtypeStruct((2048, 256), b),
            jax.ShapeDtypeStruct((8, 8, 256), jnp.float32),
        ],
        in_specs=[pl.BlockSpec(memory_space=pltpu.SMEM)] + [vm] * 6,
        out_specs=[vm] * 5,
        scratch_shapes=all_scratch(),
        compiler_params=pltpu.CompilerParams(vmem_limit_bytes=56 * 1024 * 1024),
    )(first, q, d, k, v, marks, sel)


def spread(x):
    return lax.all_to_all(x, "y", split_axis=1, concat_axis=0, tiled=True)


def gathered(x):
    return spread(lax.all_to_all(x, "head", split_axis=1, concat_axis=0, tiled=True))


def returned(x):
    return lax.all_to_all(x, "y", split_axis=0, concat_axis=1, tiled=True)


def along_z(x, by):
    n = lax.axis_size("z")
    return lax.ppermute(x, "z", [(i, (i + by) % n) for i in range(n)])


def per_device(queries, keys, values, landmarks, grad_out, selections):
    k, v = gathered(keys), gathered(values)
    kp, vp = along_z(k, 1), along_z(v, 1)
    q, d = gathered(queries), gathered(grad_out)
    mk = spread(landmarks)
    mkp = along_z(mk, 1)
    marks = jnp.concatenate([mkp, mk]).astype(jnp.float32).reshape(8, CB, HPD * HD)
    marks = jnp.concatenate([marks, jnp.zeros_like(marks)], axis=1)
    sel = lax.all_gather(selections, "y").transpose(0, 2, 1)
    sel = jnp.repeat(sel, BLOCK, axis=2)
    first = (lax.axis_index("z") - 1) * 16
    o, dq, dk, dv, dm = local_call(
        first.astype(jnp.int32).reshape(1), q, d,
        jnp.concatenate([kp, k]), jnp.concatenate([vp, v]), marks, sel)
    n = q.shape[0]
    dk = dk[n:].astype(jnp.float32) + along_z(dk[:n], -1).astype(jnp.float32)
    dv = dv[n:].astype(jnp.float32) + along_z(dv[:n], -1).astype(jnp.float32)
    dm = dm[:, :CB].reshape(32, HPD * HD)
    dm = dm[16:] + along_z(dm[:16], -1)
    b = jnp.bfloat16
    return (returned(o), returned(dq), returned(dk.astype(b)), returned(dv.astype(b)),
            returned(dm).astype(b))


def solution(mesh):
    shape = (mesh.shape["seq"] // 4, 4, mesh.shape["head"])
    split = jax.sharding.Mesh(mesh.devices.reshape(shape), ("z", "y", "head"))
    rows_all = P(("z", "y", "head"), None)
    out = P(("z", "y"), "head")
    return jax.shard_map(
        per_device, mesh=split,
        in_specs=(rows_all, rows_all, rows_all, out, rows_all, P(("z", "y"), None)),
        out_specs=(out,) * 5, check_vma=False)
```

time: 622 us -> 232 us (0.37)
  the two profiles are of different devices: /device:TPU:1 before, /device:TPU:2 now
where the time goes in v1:
time: 232 us; the launch traced here: 230 us
  waiting for transfers between devices  84.4 us (36%)
  starting transfers between devices  80.1 us (35%)
  Pallas kernels  26.2 us (11%)
  local copies, waits for them, and re-layouts  19.4 us (8%)
  blocking collectives  11.5 us (5%)
  other arithmetic  7.76 us (3%)
    all_to_all x4, waiting for transfers between devices, gathered(): lax.all_to_all(x, 'head', split_axis=1, concat_axis=0, tiled=True)  31.9 us
    all_to_all x5, waiting for transfers between devices, returned(): return lax.all_to_all(x, 'y', split_axis=0, concat_axis=1, tiled=True)  27.8 us
    pallas_call x1, Pallas kernels, local_call(): pl.pallas_call(local_kernel, out_shape=[jax.ShapeDtypeStruct((1024, 256),...  26.2 us
    all_to_all x4, starting transfers between devices, gathered(): lax.all_to_all(x, 'head', split_axis=1, concat_axis=0, tiled=True)  22.6 us
    all_to_all x5, waiting for transfers between devices, spread(): return lax.all_to_all(x, 'y', split_axis=1, concat_axis=0, tiled=True)  22 us
    ppermute x6, starting transfers between devices, along_z(): return lax.ppermute(x, 'z', [(i, (i + by) % n) for i in range(n)])  19.7 us
    all_to_all x5, starting transfers between devices, spread(): return lax.all_to_all(x, 'y', split_axis=1, concat_axis=0, tiled=True)  19.4 us
    all_to_all x5, starting transfers between devices, returned(): return lax.all_to_all(x, 'y', split_axis=0, concat_axis=1, tiled=True)  18.4 us
  transfers between devices with their start and end apart: 20, of which 14 were waited for; matrix products, arithmetic and copies ran while one was open for 10% of the time, Pallas kernels for 0%

profile of v1, /device:TPU:2, one launch (start us, length us, event | category | flops | bytes accessed | tf_op | source)
XLA Modules:
  0.0 230.3 jit_solution(3462131268955881400)
XLA Ops:
  0.6 4.5 %all-to-all-start.8 = ((bf16[4,4,256]{2,0,1:T(4,128)(2,1)}), bf16[4,4,256]{2,0,1:T(4,128)(2,1)S(1)}, u32[]{:S(2)}, u32[]{:S(2)}) async-start(bf16[4,4,256]{2,0,1:T(4,128)(2,1)} %bitcast.82), calls=%async_computation.8 | async-start | bytes 16384 | tf_op jit(solution)/shard_map/all_to_all | solution.py:167
  7.0 3.4 %all-to-all-done.8 = bf16[4,4,256]{2,0,1:T(4,128)(2,1)S(1)} async-done(((bf16[4,4,256]{2,0,1:T(4,128)(2,1)}), bf16[4,4,256]{2,0,1:T(4,128)(2,1)S(1)}, u32[]{:S(2)}, u32[]{:S(2)}) %all-to-all-start.8) | async-done | bytes 8224 | tf_op jit(solution)/shard_map/all_to_all | solution.py:167
  10.4 8.1 %all-to-all-start = ((bf16[32,8,1024]{2,0,1:T(8,128)(2,1)}), bf16[32,8,1024]{2,0,1:T(8,128)(2,1)S(1)}, u32[]{:S(2)}, u32[]{:S(2)}) async-start(bf16[32,8,1024]{2,0,1:T(8,128)(2,1)} %bitcast.55), calls=%async_computation | async-start | bytes 1048576 | tf_op jit(solution)/shard_map/all_to_all | solution.py:171
  19.3 8.1 %all-to-all-done = bf16[32,8,1024]{2,0,1:T(8,128)(2,1)S(1)} async-done(((bf16[32,8,1024]{2,0,1:T(8,128)(2,1)}), bf16[32,8,1024]{2,0,1:T(8,128)(2,1)S(1)}, u32[]{:S(2)}, u32[]{:S(2)}) %all-to-all-start) | async-done | bytes 524320 | tf_op jit(solution)/shard_map/all_to_all | solution.py:171
  27.4 4.9 %all-to-all-start.4 = ((bf16[32,8,1024]{2,0,1:T(8,128)(2,1)}), bf16[32,8,1024]{2,0,1:T(8,128)(2,1)S(1)}, u32[]{:S(2)}, u32[]{:S(2)}) async-start(bf16[32,8,1024]{2,0,1:T(8,128)(2,1)} %bitcast.53), calls=%async_computation.4 | async-start | bytes 1048576 | tf_op jit(solution)/shard_map/all_to_all | solution.py:171
  33.1 8.1 %all-to-all-done.4 = bf16[32,8,1024]{2,0,1:T(8,128)(2,1)S(1)} async-done(((bf16[32,8,1024]{2,0,1:T(8,128)(2,1)}), bf16[32,8,1024]{2,0,1:T(8,128)(2,1)S(1)}, u32[]{:S(2)}, u32[]{:S(2)}) %all-to-all-start.4) | async-done | bytes 524320 | tf_op jit(solution)/shard_map/all_to_all | solution.py:171
  41.2 4.9 %all-to-all-start.6 = ((bf16[32,8,1024]{2,0,1:T(8,128)(2,1)}), bf16[32,8,1024]{2,0,1:T(8,128)(2,1)S(1)}, u32[]{:S(2)}, u32[]{:S(2)}) async-start(bf16[32,8,1024]{2,0,1:T(8,128)(2,1)} %bitcast.52), calls=%async_computation.6 | async-start | bytes 1048576 | tf_op jit(solution)/shard_map/all_to_all | solution.py:171
  46.9 8.1 %all-to-all-done.6 = bf16[32,8,1024]{2,0,1:T(8,128)(2,1)S(1)} async-done(((bf16[32,8,1024]{2,0,1:T(8,128)(2,1)}), bf16[32,8,1024]{2,0,1:T(8,128)(2,1)S(1)}, u32[]{:S(2)}, u32[]{:S(2)}) %all-to-all-start.6) | async-done | bytes 524320 | tf_op jit(solution)/shard_map/all_to_all | solution.py:171
  54.9 4.9 %all-to-all-start.2 = ((bf16[32,8,1024]{2,0,1:T(8,128)(2,1)}), bf16[32,8,1024]{2,0,1:T(8,128)(2,1)S(1)}, u32[]{:S(2)}, u32[]{:S(2)}) async-start(bf16[32,8,1024]{2,0,1:T(8,128)(2,1)} %bitcast.54), calls=%async_computation.2 | async-start | bytes 1048576 | tf_op jit(solution)/shard_map/all_to_all | solution.py:171
  61.0 7.7 %all-to-all-done.2 = bf16[32,8,1024]{2,0,1:T(8,128)(2,1)S(1)} async-done(((bf16[32,8,1024]{2,0,1:T(8,128)(2,1)}), bf16[32,8,1024]{2,0,1:T(8,128)(2,1)S(1)}, u32[]{:S(2)}, u32[]{:S(2)}) %all-to-all-start.2) | async-done | bytes 524320 | tf_op jit(solution)/shard_map/all_to_all | solution.py:171
  68.7 3.5 %all-to-all-start.7 = ((bf16[256,4,256]{2,0,1:T(8,128)(2,1)}), bf16[256,4,256]{2,0,1:T(8,128)(2,1)S(1)}, u32[]{:S(2)}, u32[]{:S(2)}) async-start(bf16[256,4,256]{2,0,1:T(8,128)(2,1)} %copy.40), calls=%async_computation.7 | async-start | bytes 1048576 | tf_op jit(solution)/shard_map/all_to_all | solution.py:167
  73.4 8.3 %all-to-all-done.7 = bf16[256,4,256]{2,0,1:T(8,128)(2,1)S(1)} async-done(((bf16[256,4,256]{2,0,1:T(8,128)(2,1)}), bf16[256,4,256]{2,0,1:T(8,128)(2,1)S(1)}, u32[]{:S(2)}, u32[]{:S(2)}) %all-to-all-start.7) | async-done | bytes 524320 | tf_op jit(solution)/shard_map/all_to_all | solution.py:167
  81.7 3.5 %all-to-all-start.5 = ((bf16[256,4,256]{2,0,1:T(8,128)(2,1)}), bf16[256,4,256]{2,0,1:T(8,128)(2,1)S(1)}, u32[]{:S(2)}, u32[]{:S(2)}) async-start(bf16[256,4,256]{2,0,1:T(8,128)(2,1)} %copy.38), calls=%async_computation.5 | async-start | bytes 1048576 | tf_op jit(solution)/shard_map/all_to_all | solution.py:167
  88.4 5.4 %all-to-all-done.5 = bf16[256,4,256]{2,0,1:T(8,128)(2,1)S(1)} async-done(((bf16[256,4,256]{2,0,1:T(8,128)(2,1)}), bf16[256,4,256]{2,0,1:T(8,128)(2,1)S(1)}, u32[]{:S(2)}, u32[]{:S(2)}) %all-to-all-start.5) | async-done | bytes 524320 | tf_op jit(solution)/shard_map/all_to_all | solution.py:167
  93.8 3.5 %all-to-all-start.1 = ((bf16[256,4,256]{2,0,1:T(8,128)(2,1)}), bf16[256,4,256]{2,0,1:T(8,128)(2,1)S(1)}, u32[]{:S(2)}, u32[]{:S(2)}) async-start(bf16[256,4,256]{2,0,1:T(8,128)(2,1)} %copy.34), calls=%async_computation.1 | async-start | bytes 1048576 | tf_op jit(solution)/shard_map/all_to_all | solution.py:167
  99.3 2.5 %collective-permute-start.2 = (bf16[16,256]{1,0:T(8,128)(2,1)S(1)}, bf16[16,256]{1,0:T(8,128)(2,1)S(1)}, u32[]{:S(2)}, u32[]{:S(2)}) collective-permute-start(bf16[16,256]{1,0:T(8,128)(2,1)S(1)} %all_to_all.215), channel_id=1, source_target_pairs={{0,32},{32,64},{64,96},{96,128},{128,160},{160,192},{192,224},{224... | collective-permute-start | bytes 24584 | tf_op jit(solution)/shard_map/ppermute | solution.py:180
  101.8 11.5 %all-gather.1 = s32[4,4,16]{2,1,0:T(4,128)S(1)} all-gather(s32[1,4,16]{2,1,0:T(4,128)S(1)} %bitcast.83), channel_id=2, replica_groups=mesh['z'=16,'y'=4,'head'=8] {'y'}, dimensions={0}, use_global_device_ids=true | all-gather | bytes 1280 | tf_op jit(solution)/shard_map/all_gather | solution.py:191
  117.5 4.5 %all-to-all-start.3 = ((bf16[256,4,256]{2,0,1:T(8,128)(2,1)}), bf16[256,4,256]{2,0,1:T(8,128)(2,1)S(1)}, u32[]{:S(2)}, u32[]{:S(2)}) async-start(bf16[256,4,256]{2,0,1:T(8,128)(2,1)} %copy.36), calls=%async_computation.3 | async-start | bytes 1048576 | tf_op jit(solution)/shard_map/all_to_all | solution.py:167
  125.1 4.9 %all-to-all-done.3 = bf16[256,4,256]{2,0,1:T(8,128)(2,1)S(1)} async-done(((bf16[256,4,256]{2,0,1:T(8,128)(2,1)}), bf16[256,4,256]{2,0,1:T(8,128)(2,1)S(1)}, u32[]{:S(2)}, u32[]{:S(2)}) %all-to-all-start.3) | async-done | bytes 524320 | tf_op jit(solution)/shard_map/all_to_all | solution.py:167
  130.8 26.2 %shard_map.101 = (bf16[1024,256]{1,0:T(8,128)(2,1)}, bf16[1024,256]{1,0:T(8,128)(2,1)}, bf16[2048,256]{1,0:T(8,128)(2,1)}, bf16[2048,256]{1,0:T(8,128)(2,1)}, f32[8,8,256]{2,1,0:T(8,128)}) custom-call(s32[1]{0:T(128)} %bitcast.first_ref, bf16[1024,256]{1,0:T(8,128)(2,1)} %bitcast.68, bf16[1024,256]{1,0:T(8,128)(2,1)} %bitcast.69, ...), custom_call_target="tpu_custom_call" | custom-call | tf_op jit(solution)/shard_map/pallas_call | solution.py:150
  157.8 5.2 %collective-permute-start.5 = (f32[16,256]{1,0:T(8,128)S(1)}, f32[16,256]{1,0:T(8,128)S(1)}, u32[]{:S(2)}, u32[]{:S(2)}) collective-permute-start(f32[16,256]{1,0:T(8,128)S(1)} %slice.34), channel_id=1, source_target_pairs={{0,480},{32,0},{64,32},{96,64},{128,96},{160,128},{192,160},{224,1... | collective-permute-start | bytes 49160 | tf_op jit(solution)/shard_map/ppermute | solution.py:180
  165.1 3.2 %all-to-all-start.13 = ((bf16[4,4,256]{2,1,0:T(4,128)(2,1)}), bf16[4,4,256]{2,1,0:T(4,128)(2,1)S(1)}, u32[]{:S(2)}, u32[]{:S(2)}) async-start(bf16[4,4,256]{2,1,0:T(4,128)(2,1)} %all_to_all.232), calls=%async_computation.13 | async-start | bytes 16384 | tf_op jit(solution)/shard_map/all_to_all | solution.py:175
  170.3 5.4 %collective-permute-start.4 = (bf16[1024,256]{1,0:T(8,128)(2,1)}, bf16[1024,256]{1,0:T(8,128)(2,1)}, u32[]{:S(2)}, u32[]{:S(2)}) collective-permute-start(bf16[1024,256]{1,0:T(8,128)(2,1)} %slice.30), channel_id=1, source_target_pairs={{0,480},{32,0},{64,32},{96,64},{128,96},{160,128},{192,160},{224,1... | collective-permute-start | bytes 1572872 | tf_op jit(solution)/shard_map/ppermute | solution.py:180
  175.7 4.8 %all-to-all-start.10 = ((bf16[4,256,256]{2,1,0:T(8,128)(2,1)}), bf16[4,256,256]{2,1,0:T(8,128)(2,1)S(1)}, u32[]{:S(2)}, u32[]{:S(2)}) async-start(bf16[4,256,256]{2,1,0:T(8,128)(2,1)} %bitcast.19), calls=%async_computation.10 | async-start | bytes 1048576 | tf_op jit(solution)/shard_map/all_to_all | solution.py:175
  181.3 2.7 %collective-permute-start.3 = (bf16[1024,256]{1,0:T(8,128)(2,1)}, bf16[1024,256]{1,0:T(8,128)(2,1)}, u32[]{:S(2)}, u32[]{:S(2)}) collective-permute-start(bf16[1024,256]{1,0:T(8,128)(2,1)} %slice.28), channel_id=1, source_target_pairs={{0,480},{32,0},{64,32},{96,64},{128,96},{160,128},{192,160},{224,1... | collective-permute-start | bytes 1572872 | tf_op jit(solution)/shard_map/ppermute | solution.py:180
  184.1 5.7 %all-to-all-done.10 = bf16[4,256,256]{2,1,0:T(8,128)(2,1)S(1)} async-done(((bf16[4,256,256]{2,1,0:T(8,128)(2,1)}), bf16[4,256,256]{2,1,0:T(8,128)(2,1)S(1)}, u32[]{:S(2)}, u32[]{:S(2)}) %all-to-all-start.10) | async-done | bytes 524320 | tf_op jit(solution)/shard_map/all_to_all | solution.py:175
  189.8 3.5 %all-to-all-start.9 = ((bf16[4,256,256]{2,1,0:T(8,128)(2,1)}), bf16[4,256,256]{2,1,0:T(8,128)(2,1)S(1)}, u32[]{:S(2)}, u32[]{:S(2)}) async-start(bf16[4,256,256]{2,1,0:T(8,128)(2,1)} %bitcast.74), calls=%async_computation.9 | async-start | bytes 1048576 | tf_op jit(solution)/shard_map/all_to_all | solution.py:175
  195.3 8.4 %all-to-all-done.9 = bf16[4,256,256]{2,1,0:T(8,128)(2,1)S(1)} async-done(((bf16[4,256,256]{2,1,0:T(8,128)(2,1)}), bf16[4,256,256]{2,1,0:T(8,128)(2,1)S(1)}, u32[]{:S(2)}, u32[]{:S(2)}) %all-to-all-start.9) | async-done | bytes 524320 | tf_op jit(solution)/shard_map/all_to_all | solution.py:175
  203.7 3.5 %all-to-all-start.12 = ((bf16[4,256,256]{2,1,0:T(8,128)(2,1)}), bf16[4,256,256]{2,1,0:T(8,128)(2,1)S(1)}, u32[]{:S(2)}, u32[]{:S(2)}) async-start(bf16[4,256,256]{2,1,0:T(8,128)(2,1)} %bitcast.23), calls=%async_computation.12 | async-start | bytes 1048576 | tf_op jit(solution)/shard_map/all_to_all | solution.py:175
  209.2 8.1 %all-to-all-done.12 = bf16[4,256,256]{2,1,0:T(8,128)(2,1)S(1)} async-done(((bf16[4,256,256]{2,1,0:T(8,128)(2,1)}), bf16[4,256,256]{2,1,0:T(8,128)(2,1)S(1)}, u32[]{:S(2)}, u32[]{:S(2)}) %all-to-all-start.12) | async-done | bytes 524320 | tf_op jit(solution)/shard_map/all_to_all | solution.py:175
  217.3 3.5 %all-to-all-start.11 = ((bf16[4,256,256]{2,1,0:T(8,128)(2,1)}), bf16[4,256,256]{2,1,0:T(8,128)(2,1)S(1)}, u32[]{:S(2)}, u32[]{:S(2)}) async-start(bf16[4,256,256]{2,1,0:T(8,128)(2,1)} %bitcast.21), calls=%async_computation.11 | async-start | bytes 1048576 | tf_op jit(solution)/shard_map/all_to_all | solution.py:175
  223.4 5.5 %all-to-all-done.11 = bf16[4,256,256]{2,1,0:T(8,128)(2,1)S(1)} async-done(((bf16[4,256,256]{2,1,0:T(8,128)(2,1)}), bf16[4,256,256]{2,1,0:T(8,128)(2,1)S(1)}, u32[]{:S(2)}, u32[]{:S(2)}) %all-to-all-start.11) | async-done | bytes 524320 | tf_op jit(solution)/shard_map/all_to_all | solution.py:175
  (61 shorter events, 33.8 us)
Async XLA Ops:
  0.6 9.8 %all-to-all-start.8 = ((bf16[4,4,256]{2,0,1:T(4,128)(2,1)}), bf16[4,4,256]{2,0,1:T(4,128)(2,1)S(1)}, u32[]{:S(2)}, u32[]{:S(2)}) async-start(bf16[4,4,256]{2,0,1:T(4,128)(2,1)} %bitcast.82), calls=%async_computation.8 | async-start | bytes 16384 | tf_op jit(solution)/shard_map/all_to_all | solution.py:167
  5.1 13.4 %copy-start.4 = (bf16[32,8192]{1,0:T(8,128)(2,1)S(1)}, bf16[32,8192]{1,0:T(8,128)(2,1)}, u32[]{:S(2)}) copy-start(bf16[32,8192]{1,0:T(8,128)(2,1)} %param.7) | copy-start | bytes 1572868
  10.4 17.0 %all-to-all-start = ((bf16[32,8,1024]{2,0,1:T(8,128)(2,1)}), bf16[32,8,1024]{2,0,1:T(8,128)(2,1)S(1)}, u32[]{:S(2)}, u32[]{:S(2)}) async-start(bf16[32,8,1024]{2,0,1:T(8,128)(2,1)} %bitcast.55), calls=%async_computation | async-start | bytes 1048576 | tf_op jit(solution)/shard_map/all_to_all | solution.py:171
  18.5 13.8 %copy-start.5 = (bf16[32,8192]{1,0:T(8,128)(2,1)S(1)}, bf16[32,8192]{1,0:T(8,128)(2,1)}, u32[]{:S(2)}) copy-start(bf16[32,8192]{1,0:T(8,128)(2,1)} %param.8) | copy-start | bytes 1572868
  27.4 13.8 %all-to-all-start.4 = ((bf16[32,8,1024]{2,0,1:T(8,128)(2,1)}), bf16[32,8,1024]{2,0,1:T(8,128)(2,1)S(1)}, u32[]{:S(2)}, u32[]{:S(2)}) async-start(bf16[32,8,1024]{2,0,1:T(8,128)(2,1)} %bitcast.53), calls=%async_computation.4 | async-start | bytes 1048576 | tf_op jit(solution)/shard_map/all_to_all | solution.py:171
  32.3 13.8 %copy-start.6 = (bf16[32,8192]{1,0:T(8,128)(2,1)S(1)}, bf16[32,8192]{1,0:T(8,128)(2,1)}, u32[]{:S(2)}) copy-start(bf16[32,8192]{1,0:T(8,128)(2,1)} %param.10) | copy-start | bytes 1572868
  41.2 13.8 %all-to-all-start.6 = ((bf16[32,8,1024]{2,0,1:T(8,128)(2,1)}), bf16[32,8,1024]{2,0,1:T(8,128)(2,1)S(1)}, u32[]{:S(2)}, u32[]{:S(2)}) async-start(bf16[32,8,1024]{2,0,1:T(8,128)(2,1)} %bitcast.52), calls=%async_computation.6 | async-start | bytes 1048576 | tf_op jit(solution)/shard_map/all_to_all | solution.py:171
  54.9 13.8 %all-to-all-start.2 = ((bf16[32,8,1024]{2,0,1:T(8,128)(2,1)}), bf16[32,8,1024]{2,0,1:T(8,128)(2,1)S(1)}, u32[]{:S(2)}, u32[]{:S(2)}) async-start(bf16[32,8,1024]{2,0,1:T(8,128)(2,1)} %bitcast.54), calls=%async_computation.2 | async-start | bytes 1048576 | tf_op jit(solution)/shard_map/all_to_all | solution.py:171
  68.7 13.0 %all-to-all-start.7 = ((bf16[256,4,256]{2,0,1:T(8,128)(2,1)}), bf16[256,4,256]{2,0,1:T(8,128)(2,1)S(1)}, u32[]{:S(2)}, u32[]{:S(2)}) async-start(bf16[256,4,256]{2,0,1:T(8,128)(2,1)} %copy.40), calls=%async_computation.7 | async-start | bytes 1048576 | tf_op jit(solution)/shard_map/all_to_all | solution.py:167
  81.7 12.1 %all-to-all-start.5 = ((bf16[256,4,256]{2,0,1:T(8,128)(2,1)}), bf16[256,4,256]{2,0,1:T(8,128)(2,1)S(1)}, u32[]{:S(2)}, u32[]{:S(2)}) async-start(bf16[256,4,256]{2,0,1:T(8,128)(2,1)} %copy.38), calls=%async_computation.5 | async-start | bytes 1048576 | tf_op jit(solution)/shard_map/all_to_all | solution.py:167
  85.2 36.8 %collective-permute-start.1 = (bf16[1024,256]{1,0:T(8,128)(2,1)S(1)}, bf16[1024,256]{1,0:T(8,128)(2,1)S(1)}, u32[]{:S(2)}, u32[]{:S(2)}) collective-permute-start(bf16[1024,256]{1,0:T(8,128)(2,1)S(1)} %bitcast.64), channel_id=1, source_target_pairs={{0,32},{32,64},{64,96},{96,128},{128,160},{160,192},{192,224},{224... | collective-permute-start | bytes 1572872 | tf_op jit(solution)/shard_map/ppermute | solution.py:180
  87.5 14.2 %copy-start.7 = (s32[4,16]{1,0:T(4,128)S(1)}, s32[4,16]{1,0:T(4,128)}, u32[]{:S(2)}) copy-start(s32[4,16]{1,0:T(4,128)} %param.11) | copy-start | bytes 772
  93.8 23.7 %all-to-all-start.1 = ((bf16[256,4,256]{2,0,1:T(8,128)(2,1)}), bf16[256,4,256]{2,0,1:T(8,128)(2,1)S(1)}, u32[]{:S(2)}, u32[]{:S(2)}) async-start(bf16[256,4,256]{2,0,1:T(8,128)(2,1)} %copy.34), calls=%async_computation.1 | async-start | bytes 1048576 | tf_op jit(solution)/shard_map/all_to_all | solution.py:167
  97.3 25.7 %collective-permute-start = (bf16[1024,256]{1,0:T(8,128)(2,1)S(1)}, bf16[1024,256]{1,0:T(8,128)(2,1)}, u32[]{:S(2)}, u32[]{:S(2)}) collective-permute-start(bf16[1024,256]{1,0:T(8,128)(2,1)S(1)} %bitcast.66), channel_id=1, source_target_pairs={{0,32},{32,64},{64,96},{96,128},{128,160},{160,192},{192,224},{224... | collective-permute-start | bytes 1572872 | tf_op jit(solution)/shard_map/ppermute | solution.py:180
  99.3 16.4 %collective-permute-start.2 = (bf16[16,256]{1,0:T(8,128)(2,1)S(1)}, bf16[16,256]{1,0:T(8,128)(2,1)S(1)}, u32[]{:S(2)}, u32[]{:S(2)}) collective-permute-start(bf16[16,256]{1,0:T(8,128)(2,1)S(1)} %all_to_all.215), channel_id=1, source_target_pairs={{0,32},{32,64},{64,96},{96,128},{128,160},{160,192},{192,224},{224... | collective-permute-start | bytes 24584 | tf_op jit(solution)/shard_map/ppermute | solution.py:180
  117.5 5.5 %copy-start = (bf16[256,4,256]{2,0,1:T(8,128)(2,1)}, bf16[256,4,256]{2,0,1:T(8,128)(2,1)S(1)}, u32[]{:S(2)}) copy-start(bf16[256,4,256]{2,0,1:T(8,128)(2,1)S(1)} %all-to-all-done.1) | copy-start | bytes 1572868
  117.5 12.6 %all-to-all-start.3 = ((bf16[256,4,256]{2,0,1:T(8,128)(2,1)}), bf16[256,4,256]{2,0,1:T(8,128)(2,1)S(1)}, u32[]{:S(2)}, u32[]{:S(2)}) async-start(bf16[256,4,256]{2,0,1:T(8,128)(2,1)} %copy.36), calls=%async_computation.3 | async-start | bytes 1048576 | tf_op jit(solution)/shard_map/all_to_all | solution.py:167
  130.1 0.8 copy-start.1
  157.8 6.7 %collective-permute-start.5 = (f32[16,256]{1,0:T(8,128)S(1)}, f32[16,256]{1,0:T(8,128)S(1)}, u32[]{:S(2)}, u32[]{:S(2)}) collective-permute-start(f32[16,256]{1,0:T(8,128)S(1)} %slice.34), channel_id=1, source_target_pairs={{0,480},{32,0},{64,32},{96,64},{128,96},{160,128},{192,160},{224,1... | collective-permute-start | bytes 49160 | tf_op jit(solution)/shard_map/ppermute | solution.py:180
  165.1 10.6 %all-to-all-start.13 = ((bf16[4,4,256]{2,1,0:T(4,128)(2,1)}), bf16[4,4,256]{2,1,0:T(4,128)(2,1)S(1)}, u32[]{:S(2)}, u32[]{:S(2)}) async-start(bf16[4,4,256]{2,1,0:T(4,128)(2,1)} %all_to_all.232), calls=%async_computation.13 | async-start | bytes 16384 | tf_op jit(solution)/shard_map/all_to_all | solution.py:175
  168.4 12.2 %copy-start.2 = (bf16[2048,256]{1,0:T(8,128)(2,1)S(1)}, bf16[2048,256]{1,0:T(8,128)(2,1)}, u32[]{:S(2)}) copy-start(bf16[2048,256]{1,0:T(8,128)(2,1)} %get-tuple-element.12) | copy-start | bytes 3145732
  170.3 22.9 %collective-permute-start.4 = (bf16[1024,256]{1,0:T(8,128)(2,1)}, bf16[1024,256]{1,0:T(8,128)(2,1)}, u32[]{:S(2)}, u32[]{:S(2)}) collective-permute-start(bf16[1024,256]{1,0:T(8,128)(2,1)} %slice.30), channel_id=1, source_target_pairs={{0,480},{32,0},{64,32},{96,64},{128,96},{160,128},{192,160},{224,1... | collective-permute-start | bytes 1572872 | tf_op jit(solution)/shard_map/ppermute | solution.py:180
  175.7 14.0 %all-to-all-start.10 = ((bf16[4,256,256]{2,1,0:T(8,128)(2,1)}), bf16[4,256,256]{2,1,0:T(8,128)(2,1)S(1)}, u32[]{:S(2)}, u32[]{:S(2)}) async-start(bf16[4,256,256]{2,1,0:T(8,128)(2,1)} %bitcast.19), calls=%async_computation.10 | async-start | bytes 1048576 | tf_op jit(solution)/shard_map/all_to_all | solution.py:175
  180.5 12.8 %copy-start.3 = (bf16[2048,256]{1,0:T(8,128)(2,1)S(1)}, bf16[2048,256]{1,0:T(8,128)(2,1)}, u32[]{:S(2)}) copy-start(bf16[2048,256]{1,0:T(8,128)(2,1)} %get-tuple-element.13) | copy-start | bytes 3145732
  181.3 25.9 %collective-permute-start.3 = (bf16[1024,256]{1,0:T(8,128)(2,1)}, bf16[1024,256]{1,0:T(8,128)(2,1)}, u32[]{:S(2)}, u32[]{:S(2)}) collective-permute-start(bf16[1024,256]{1,0:T(8,128)(2,1)} %slice.28), channel_id=1, source_target_pairs={{0,480},{32,0},{64,32},{96,64},{128,96},{160,128},{192,160},{224,1... | collective-permute-start | bytes 1572872 | tf_op jit(solution)/shard_map/ppermute | solution.py:180
  189.8 13.9 %all-to-all-start.9 = ((bf16[4,256,256]{2,1,0:T(8,128)(2,1)}), bf16[4,256,256]{2,1,0:T(8,128)(2,1)S(1)}, u32[]{:S(2)}, u32[]{:S(2)}) async-start(bf16[4,256,256]{2,1,0:T(8,128)(2,1)} %bitcast.74), calls=%async_computation.9 | async-start | bytes 1048576 | tf_op jit(solution)/shard_map/all_to_all | solution.py:175
  203.7 13.6 %all-to-all-start.12 = ((bf16[4,256,256]{2,1,0:T(8,128)(2,1)}), bf16[4,256,256]{2,1,0:T(8,128)(2,1)S(1)}, u32[]{:S(2)}, u32[]{:S(2)}) async-start(bf16[4,256,256]{2,1,0:T(8,128)(2,1)} %bitcast.23), calls=%async_computation.12 | async-start | bytes 1048576 | tf_op jit(solution)/shard_map/all_to_all | solution.py:175
  217.3 11.5 %all-to-all-start.11 = ((bf16[4,256,256]{2,1,0:T(8,128)(2,1)}), bf16[4,256,256]{2,1,0:T(8,128)(2,1)S(1)}, u32[]{:S(2)}, u32[]{:S(2)}) async-start(bf16[4,256,256]{2,1,0:T(8,128)(2,1)} %bitcast.21), calls=%async_computation.11 | async-start | bytes 1048576 | tf_op jit(solution)/shard_map/all_to_all | solution.py:175

commit v2 on v1

v2 whole, which is shorter than its diff:
```python
import jax
import jax.numpy as jnp
from jax import lax
from jax.experimental import pallas as pl
from jax.experimental.pallas import tpu as pltpu
from jax.sharding import PartitionSpec as P

HD = 128
BLOCK = 64
HPD = 2
CH = 256
CB = CH // BLOCK
SCALE = HD ** (-0.5)
LOG2E = 1.4426950408889634
NT = (((1,), (1,)), ((), ()))
NN = (((1,), (0,)), ((), ()))
TN = (((0,), (0,)), ((), ()))


def dot(a, b, dims):
    return lax.dot_general(a, b, dims, preferred_element_type=jnp.float32)


def rows(c):
    return pl.ds(pl.multiple_of(c * CH, CH), CH)


def lanes(h):
    return slice(h * HD, (h + 1) * HD)


def gate_tile(t, first, q, marks, sel, gates):
    row = lax.broadcasted_iota(jnp.int32, (64, CH), 0)
    sub = row % 8
    block = first + (row // 8) * CB + sub
    block = jnp.where((sub < CB) & (block >= 0), block, -2)
    picks = sel[t]
    live = block == picks[0:1]
    for e in range(1, picks.shape[0]):
        live = live | (block == picks[e:e + 1])
    for h in range(HPD):
        mk = marks[:, :, lanes(h)].reshape(64, HD).astype(jnp.bfloat16)
        coarse = dot(mk, q[rows(t), lanes(h)], NT) * SCALE
        coarse = jnp.where(live, coarse, -1e30)
        top = jnp.max(coarse, axis=0, keepdims=True)
        ex = jnp.exp(coarse - top)
        gates[h, t] = (ex / jnp.sum(ex, axis=0, keepdims=True)).reshape(8, 8, CH)


def cell(t, kc, diag, q, d, k, v, kt, vt, gates, dgates, ot, dqt, dk, dv):
    for h in range(HPD):
        qh = q[rows(t), lanes(h)]
        dh = d[rows(t), lanes(h)]
        s = dot(k[rows(kc), lanes(h)], qh, NT)
        g = dot(v[rows(kc), lanes(h)], dh, NT)
        if diag:
            j = lax.broadcasted_iota(jnp.int32, (CH, CH), 0)
            i = lax.broadcasted_iota(jnp.int32, (CH, CH), 1)
            s = jnp.where(j > i, -1e30, s)
        s = s.reshape(CB, BLOCK, CH)
        g = g.reshape(CB, BLOCK, CH)
        top = jnp.max(s, axis=1, keepdims=True)
        p = jnp.exp2((s - top) * (SCALE * LOG2E))
        rz = 1.0 / jnp.sum(p, axis=1, keepdims=True)
        dg = jnp.sum(p * g, axis=1, keepdims=True) * rz
        gate = gates[h, t, kc][0:CB].reshape(CB, 1, CH)
        w = p * (gate * rz)
        ds = w * (g - dg)
        dgates[h, t, kc, 0:CB] = dg.reshape(CB, CH)
        wb = w.astype(jnp.bfloat16).reshape(CH, CH)
        sb = ds.astype(jnp.bfloat16).reshape(CH, CH)
        ot[h, t] += dot(vt[h, kc], wb, NN)
        dqt[h, t] += dot(kt[h, kc], sb, NN)
        dv[kc, :, lanes(h)] += dot(wb, dh, NN)
        dk[kc, :, lanes(h)] += dot(sb, qh, NN)


def transpose_chunk(kc, src, dst):
    for h in range(HPD):
        dst[h, kc] = src[rows(kc), lanes(h)].T


def close_tile(t, q, marks, gates, dgates, ot, dqt, dm, o_out, dq_out):
    for h in range(HPD):
        gate = gates[h, t].reshape(64, CH)
        dg = dgates[h, t].reshape(64, CH)
        dc = gate * (dg - jnp.sum(gate * dg, axis=0, keepdims=True))
        dcb = dc.astype(jnp.bfloat16)
        mk = marks[:, :, lanes(h)].reshape(64, HD).astype(jnp.bfloat16)
        dq = dqt[h, t] + dot(mk, dcb, TN)
        o_out[t, :, lanes(h)] = ot[h, t].T.astype(jnp.bfloat16)
        dq_out[t, :, lanes(h)] = (dq * SCALE).T.astype(jnp.bfloat16)
        dm[:, :, lanes(h)] += (dot(dcb, q[rows(t), lanes(h)], NN) * SCALE).reshape(8, 8, HD)


def all_scratch():
    f = jnp.float32
    return [
        pltpu.VMEM((HPD, 8, HD, CH), jnp.bfloat16),
        pltpu.VMEM((HPD, 8, HD, CH), jnp.bfloat16),
        pltpu.VMEM((HPD, 4, 8, 8, CH), f),
        pltpu.VMEM((HPD, 4, 8, 8, CH), f),
        pltpu.VMEM((HPD, 4, HD, CH), f),
        pltpu.VMEM((HPD, 4, HD, CH), f),
        pltpu.VMEM((8, CH, HPD * HD), f),
        pltpu.VMEM((8, CH, HPD * HD), f),
    ]


MESH = pl.DeviceIdType.MESH
NY = 4
K, V, Q, D = 0, 1, 2, 3


def remote(src, dst, send, recv, **where):
    return pltpu.make_async_remote_copy(
        src_ref=src, dst_ref=dst, send_sem=send, recv_sem=recv, device_id=where, device_id_type=MESH)


def kernel(nz, nh, k_in, v_in, q_in, d_in, marks_in, sel_in,
           o_out, dq_out, dk_out, dv_out, dm_out,
           xb, k_win, v_win, q_all, d_all, marks, sel, gsend, gback, osend, dm, dmback, dmsend,
           kt, vt, gates, dgates, ot, dqt, dk, dv,
           x_loc, x_send, x_recv, y_loc, y_send, y_recv, z_send, z_recv,
           s_loc, s_send, s_recv, mz_send, mz_recv, g_send, g_recv, gm_send, gm_recv,
           o_loc, o_send, o_recv):
    z, y, h = lax.axis_index("z"), lax.axis_index("y"), lax.axis_index("head")
    up, down = lax.rem(z + 1, nz), lax.rem(z + nz - 1, nz)
    inputs = (k_in, v_in, q_in, d_in)
    wide = xb.shape[2]
    part = k_in.shape[0]

    def to_y(k):
        return lax.rem(y + k, NY)

    def from_y(k):
        return lax.rem(y + NY - k, NY)

    def cols(c):
        return pl.ds(pl.multiple_of(c * CH, CH), CH)

    barrier = pltpu.get_barrier_semaphore()
    for k in range(1, nh):
        pl.semaphore_signal(barrier, inc=1, device_id={"head": lax.rem(h + k, nh)}, device_id_type=MESH)
    for k in range(1, NY):
        pl.semaphore_signal(barrier, inc=1, device_id={"y": to_y(k)}, device_id_type=MESH)
    for other in (up, down):
        pl.semaphore_signal(barrier, inc=1, device_id={"z": other}, device_id_type=MESH)
    pl.semaphore_wait(barrier, nh + NY)

    def x_copies(a):
        out = []
        mine = pl.ds(pl.multiple_of(h * part, part), part)
        for k in range(1, nh):
            to = lax.rem(h + k, nh)
            out.append(remote(
                inputs[a].at[:, pl.ds(pl.multiple_of(to * wide, wide), wide)],
                xb.at[a, mine, :], x_send.at[a, k], x_recv.at[a, k], head=to))
        return out

    def x_local(a):
        mine = pl.ds(pl.multiple_of(h * part, part), part)
        return pltpu.make_async_copy(
            inputs[a].at[:, pl.ds(pl.multiple_of(h * wide, wide), wide)], xb.at[a, mine, :], x_loc.at[a])

    def x_start(a):
        for c in x_copies(a):
            c.start()
        x_local(a).start()

    def x_wait(a):
        for c in x_copies(a):
            c.wait_recv()
        x_local(a).wait()

    def own_rows(a, c):
        if a == K:
            return k_win.at[rows(NY + c), :]
        if a == V:
            return v_win.at[rows(NY + c), :]
        return (q_all if a == Q else d_all).at[rows(c), :]

    def y_copy(a, k):
        to = to_y(k)
        return remote(xb.at[a, :, cols(to)], own_rows(a, y), y_send.at[a, k], y_recv.at[a, k], y=to)

    def y_arrival(a, k):
        return remote(xb.at[a, :, cols(y)], own_rows(a, from_y(k)), y_send.at[a, k], y_recv.at[a, k], y=y)

    def y_local(a):
        return pltpu.make_async_copy(xb.at[a, :, cols(y)], own_rows(a, y), y_loc.at[a])

    def y_start(a):
        for k in range(1, NY):
            y_copy(a, k).start()
        y_local(a).start()

    def z_copy(a, k):
        win = (k_win, v_win)[a]
        c = from_y(k)
        src = xb.at[a, :, cols(y)] if k == 0 else win.at[rows(NY + c), :]
        return remote(src, win.at[rows(c), :], z_send.at[a, k], z_recv.at[a, k], z=up)

    mark_loc = pltpu.make_async_copy(marks_in.at[:, cols(y)], marks.at[NY + y], s_loc.at[0])
    sel_loc = pltpu.make_async_copy(sel_in, sel.at[y], s_loc.at[1])

    def mark_copy(k):
        to = to_y(k)
        return remote(marks_in.at[:, cols(to)], marks.at[NY + y], s_send.at[0, k], s_recv.at[0, k], y=to)

    def mark_arrival(k):
        return remote(marks_in.at[:, cols(y)], marks.at[NY + from_y(k)], s_send.at[0, k], s_recv.at[0, k], y=y)

    def sel_copy(k):
        return remote(sel_in, sel.at[y], s_send.at[1, k], s_recv.at[1, k], y=to_y(k))

    def sel_arrival(k):
        return remote(sel_in, sel.at[from_y(k)], s_send.at[1, k], s_recv.at[1, k], y=y)

    mark_up = remote(marks.at[pl.ds(NY, NY)], marks.at[pl.ds(0, NY)], mz_send, mz_recv, z=up)

    mark_loc.start()
    sel_loc.start()
    for k in range(1, NY):
        mark_copy(k).start()
        sel_copy(k).start()
    x_start(K)
    x_start(V)

    ot[...] = jnp.zeros_like(ot)
    dqt[...] = jnp.zeros_like(dqt)
    dk[...] = jnp.zeros_like(dk)
    dv[...] = jnp.zeros_like(dv)
    dgates[...] = jnp.zeros_like(dgates)
    dm[...] = jnp.zeros_like(dm)

    mark_loc.wait()
    sel_loc.wait()
    for k in range(1, NY):
        mark_arrival(k).wait_recv()
        sel_arrival(k).wait_recv()
    mark_up.start()

    for a, following in ((K, Q), (V, D)):
        x_wait(a)
        y_start(a)
        z_copy(a, 0).start()
        x_start(following)
    for a in (K, V):
        for k in range(1, NY):
            y_arrival(a, k).wait_recv()
            z_copy(a, k).start()
        y_local(a).wait()
    mark_up.wait_recv()

    @pl.loop(NY, 2 * NY)
    def _(kc):
        transpose_chunk(kc, k_win, kt)
        transpose_chunk(kc, v_win, vt)

    x_wait(Q)
    y_start(Q)
    x_wait(D)
    y_start(D)
    for k in range(1, NY):
        y_arrival(Q, k).wait_recv()
    y_local(Q).wait()

    first = (z - 1) * (NY * CB)

    @pl.loop(0, NY)
    def _(t):
        gate_tile(t, first, q_all, marks, sel, gates)

    for k in range(1, NY):
        y_arrival(D, k).wait_recv()
    y_local(D).wait()

    args = (q_all, d_all, k_win, v_win, kt, vt, gates, dgates, ot, dqt, dk, dv)

    @pl.loop(0, NY)
    def _(c):
        cell(c, c + NY, True, *args)

        @pl.loop(c + 1, NY)
        def _(t):
            cell(t, c + NY, False, *args)

    def arrival(a, k):
        win = (k_win, v_win)[a]
        return remote(win.at[rows(NY), :], win.at[rows(from_y(k)), :], z_send.at[a, k], z_recv.at[a, k], z=up)

    def g_copy(a, k):
        c = from_y(k)
        return remote(gsend.at[a, c], gback.at[a, c], g_send.at[a, k], g_recv.at[a, k], z=down)

    @pl.loop(0, NY)
    def _(k):
        c = from_y(k)
        arrival(K, k).wait_recv()
        arrival(V, k).wait_recv()
        transpose_chunk(c, k_win, kt)
        transpose_chunk(c, v_win, vt)

        @pl.loop(0, c + 1)
        def _(t):
            cell(t, c, False, *args)

        gsend[K, c] = (dk[c] * SCALE).astype(jnp.bfloat16)
        g_copy(K, k).start()
        gsend[V, c] = dv[c].astype(jnp.bfloat16)
        g_copy(V, k).start()

    outs = (dk_out, dv_out, o_out, dq_out)

    def o_copy(a, k):
        to = from_y(k)
        return remote(osend.at[a, to], outs[a].at[:, cols(y)], o_send.at[a, k], o_recv.at[a, k], y=to)

    def o_arrival(a, k):
        return remote(osend.at[a, 0], outs[a].at[:, cols(to_y(k))], o_send.at[a, k], o_recv.at[a, k], y=y)

    def o_local(a):
        return pltpu.make_async_copy(osend.at[a, y], outs[a].at[:, cols(y)], o_loc.at[a])

    def o_start(a, k):
        if k == 0:
            o_local(a).start()
        else:
            o_copy(a, k).start()

    for k in (1, 2, 3, 0):
        t = from_y(k)
        close_tile(t, q_all, marks, gates, dgates, ot, dqt, dm, osend.at[Q], osend.at[D])
        o_start(Q, k)
        o_start(D, k)

    dmsend[...] = dm[0:NY]
    dm_back = remote(dmsend, dmback, gm_send, gm_recv, z=down)
    dm_back.start()

    for k in range(NY):
        c = from_y(k)
        g_copy(K, k).wait_recv()
        osend[K, c] = (dk[NY + c] * SCALE + gback[K, c].astype(jnp.float32)).astype(jnp.bfloat16)
        o_start(K, k)
        g_copy(V, k).wait_recv()
        osend[V, c] = (dv[NY + c] + gback[V, c].astype(jnp.float32)).astype(jnp.bfloat16)
        o_start(V, k)

    dm_back.wait_recv()
    dm[NY:] = dm[NY:] + dmback[...]

    def dm_copy(k):
        to = from_y(k)
        return remote(dm.at[NY + to], dm_out.at[:, cols(y)], o_send.at[4, k], o_recv.at[4, k], y=to)

    def dm_arrival(k):
        return remote(dm.at[NY], dm_out.at[:, cols(to_y(k))], o_send.at[4, k], o_recv.at[4, k], y=y)

    dm_local = pltpu.make_async_copy(dm.at[NY + y], dm_out.at[:, cols(y)], o_loc.at[4])
    for k in range(1, NY):
        dm_copy(k).start()
    dm_local.start()

    for a in range(4):
        for c in x_copies(a):
            c.wait_send()
        for k in range(1, NY):
            y_copy(a, k).wait_send()
            o_copy(a, k).wait_send()
            o_arrival(a, k).wait_recv()
        o_local(a).wait()
    for k in range(1, NY):
        mark_copy(k).wait_send()
        sel_copy(k).wait_send()
        dm_copy(k).wait_send()
        dm_arrival(k).wait_recv()
    dm_local.wait()
    for a in (K, V):
        for k in range(NY):
            z_copy(a, k).wait_send()
            g_copy(a, k).wait_send()
    mark_up.wait_send()
    dm_back.wait_send()


def per_device(queries, keys, values, landmarks, grad_out, selections):
    nz, nh = lax.axis_size("z"), lax.axis_size("head")
    width = landmarks.shape[1]
    marks = jnp.concatenate([landmarks.astype(jnp.float32), jnp.zeros((8 - CB, width), jnp.float32)])
    sel = jnp.repeat(selections.T, BLOCK, axis=1)
    b, f = jnp.bfloat16, jnp.float32
    hbm = pl.BlockSpec(memory_space=pl.ANY)
    big = jax.ShapeDtypeStruct((CH, width), b)
    tall = NY * CH
    feat = HPD * HD
    sem = pltpu.SemaphoreType.DMA
    o, dq, dk, dv, dm = pl.pallas_call(
        lambda *refs: kernel(nz, nh, *refs),
        out_shape=[big] * 4 + [jax.ShapeDtypeStruct((8, width), f)],
        in_specs=[hbm] * 6,
        out_specs=[hbm] * 5,
        scratch_shapes=[
            pltpu.VMEM((4, CH, width), b),
            pltpu.VMEM((2 * tall, feat), b),
            pltpu.VMEM((2 * tall, feat), b),
            pltpu.VMEM((tall, feat), b),
            pltpu.VMEM((tall, feat), b),
            pltpu.VMEM((8, 8, feat), f),
            pltpu.VMEM((NY, selections.shape[1], CH), jnp.int32),
            pltpu.VMEM((2, NY, CH, feat), b),
            pltpu.VMEM((2, NY, CH, feat), b),
            pltpu.VMEM((4, NY, CH, feat), b),
            pltpu.VMEM((8, 8, feat), f),
            pltpu.VMEM((NY, 8, feat), f),
            pltpu.VMEM((NY, 8, feat), f),
        ] + all_scratch() + [
            sem((4,)), sem((4, 8)), sem((4, 8)),
            sem((4,)), sem((4, 4)), sem((4, 4)),
            sem((2, 4)), sem((2, 4)),
            sem((2,)), sem((2, 4)), sem((2, 4)),
            sem, sem,
            sem((2, 4)), sem((2, 4)), sem, sem,
            sem((5,)), sem((5, 4)), sem((5, 4)),
        ],
        compiler_params=pltpu.CompilerParams(
            collective_id=0, has_side_effects=True, vmem_limit_bytes=48 * 1024 * 1024),
    )(keys, values, queries, grad_out, marks, sel)
    return o, dq, dk, dv, dm[:CB].astype(b)


def solution(mesh):
    shape = (mesh.shape["seq"] // NY, NY, mesh.shape["head"])
    split = jax.sharding.Mesh(mesh.devices.reshape(shape), ("z", "y", "head"))
    rows_all = P(("z", "y", "head"), None)
    out = P(("z", "y"), "head")
    return jax.shard_map(
        per_device, mesh=split,
        in_specs=(rows_all, rows_all, rows_all, out, rows_all, P(("z", "y"), None)),
        out_specs=(out,) * 5, check_vma=False)
```

time: 232 us -> 107 us (0.46)
  the two profiles are of different devices: /device:TPU:2 before, /device:TPU:1 now
where the time goes in v2:
time: 107 us
  Pallas kernels  96.9 us (91%)
  local copies, waits for them, and re-layouts  9.47 us (9%)
    pallas_call x1, Pallas kernels, per_device(): pl.pallas_call(lambda *refs: kernel(nz, nh, *refs), out_shape=[big] * 4 +...  96.9 us
    unnamed x14, local copies, waits for them, and re-layouts  7.94 us

profile of v2, /device:TPU:1, one launch (start us, length us, event | category | flops | bytes accessed | tf_op | source)
XLA Modules:
  0.0 107.0 jit_solution(7557357997765688258)
XLA Ops:
  0.6 0.8 copy.11
  1.4 0.1 broadcast_in_dim.4
  1.5 0.0 copy-start.4
  1.5 0.1 reshape.13.refs_5_
  1.6 0.6 copy-done.4
  2.2 0.0 copy-start
  2.2 1.0 copy-done
  3.2 0.0 copy-start.1
  3.2 1.0 copy-done.1
  4.3 0.0 copy-start.2
  4.3 1.0 copy-done.2
  5.3 0.0 copy-start.3
  5.3 1.0 copy-done.3
  6.3 96.9 %shard_map.101 = (bf16[256,1024]{1,0:T(8,128)(2,1)S(1)}, bf16[256,1024]{1,0:T(8,128)(2,1)S(1)}, bf16[256,1024]{1,0:T(8,128)(2,1)S(1)}, bf16[256,1024]{1,0:T(8,128)(2,1)S(1)}, f32[8,1024]{1,0:T(8,128)S(1)}) custom-call(bf16[32,8192]{1,0:T(8,128)(2,1)S(1)} %copy-done, bf16[32,8192]{1,0:T(8,128)(2,1)S(1)} %copy-done.1, bf16[32,8192]{1,0:T(8,128)(2,1)S(1)} %copy-done.2, ...), custom_call_target="tpu_custom_call" | custom-call | tf_op jit(solution)/shard_map/pallas_call | solution.py:399
  103.2 0.6 slice.7
  103.8 0.8 copy.16
  104.6 0.8 copy.17
  105.4 0.8 copy.18
  106.2 0.8 copy.19
  (1 shorter events, 0.0 us)
Async XLA Ops:
  1.5 0.7 copy-start.4
  2.2 1.0 copy-start
  3.2 1.0 copy-start.1
  4.3 1.0 copy-start.2
  5.3 1.0 copy-start.3

commit v3 on v1

v3 whole, which is shorter than its diff:
```python
import jax
import jax.numpy as jnp
from jax import lax
from jax.experimental import pallas as pl
from jax.experimental.pallas import tpu as pltpu
from jax.sharding import PartitionSpec as P

HD = 128
BLOCK = 64
HPD = 2
CH = 256
CB = CH // BLOCK
NY = 4
SCALE = HD ** (-0.5)
LOG2E = 1.4426950408889634
NT = (((1,), (1,)), ((), ()))
NN = (((1,), (0,)), ((), ()))
TN = (((0,), (0,)), ((), ()))
MESH = pl.DeviceIdType.MESH
K, V, Q, D = 0, 1, 2, 3


def dot(a, b, dims):
    return lax.dot_general(a, b, dims, preferred_element_type=jnp.float32)


def rows(c):
    return pl.ds(pl.multiple_of(c * CH, CH), CH)


def gate_tile(s, t, first, q, marks, sel, gates):
    row = lax.broadcasted_iota(jnp.int32, (64, CH), 0)
    sub = row % 8
    block = first + (row // 8) * CB + sub
    block = jnp.where((sub < CB) & (block >= 0), block, -2).astype(jnp.float32)
    picks = sel[t]
    live = block == picks[0:1]
    for e in range(1, picks.shape[0]):
        live = live | (block == picks[e:e + 1])
    mk = marks[:, :, s * HD:(s + 1) * HD].reshape(64, HD).astype(jnp.bfloat16)
    coarse = dot(mk, q[s, rows(t), :], NT) * SCALE
    coarse = jnp.where(live, coarse, -1e30)
    top = jnp.max(coarse, axis=0, keepdims=True)
    ex = jnp.exp(coarse - top)
    gates[s, t] = (ex / jnp.sum(ex, axis=0, keepdims=True)).reshape(8, 8, CH)


def chunk_cells(h, c, q, d, k, v, kt, vt, gates, dgates, ot, dqt, dk, dv):
    cells = [(t, jnp.where(t <= c, c, c + NY), False) for t in range(NY)] + [(c, c + NY, True)]

    def first(i):
        t, kc, _ = cells[i]
        return (dot(k[h, rows(kc), :], q[h, rows(t), :], NT), dot(v[h, rows(kc), :], d[h, rows(t), :], NT))

    def middle(i, s, g):
        t, kc, diag = cells[i]
        if diag:
            row = lax.broadcasted_iota(jnp.int32, (CH, CH), 0)
            col = lax.broadcasted_iota(jnp.int32, (CH, CH), 1)
            s = jnp.where(row > col, -1e30, s)
        s = s.reshape(CB, BLOCK, CH)
        g = g.reshape(CB, BLOCK, CH)
        top = jnp.max(s, axis=1, keepdims=True)
        p = jnp.exp2((s - top) * (SCALE * LOG2E))
        rz = 1.0 / jnp.sum(p, axis=1, keepdims=True)
        dg = jnp.sum(p * g, axis=1, keepdims=True) * rz
        gate = gates[h, t, kc][0:CB].reshape(CB, 1, CH)
        w = p * (gate * rz)
        ds = w * (g - dg)
        dgates[h, t, kc, 0:CB] = dg.reshape(CB, CH)
        return w.astype(jnp.bfloat16).reshape(CH, CH), ds.astype(jnp.bfloat16).reshape(CH, CH)

    def last(i, wb, sb):
        t, kc, _ = cells[i]
        ot[h, t] += dot(vt[h, kc], wb, NN)
        dqt[h, t] += dot(kt[h, kc], sb, NN)
        dv[h, kc] += dot(wb, d[h, rows(t), :], NN)
        dk[h, kc] += dot(sb, q[h, rows(t), :], NN)

    ready, done = first(0), None
    for i in range(len(cells)):
        following = first(i + 1) if i + 1 < len(cells) else None
        pair = middle(i, *ready)
        if done is not None:
            last(i - 1, *done)
        ready, done = following, pair
    last(len(cells) - 1, *done)


def close_tile(s, t, q, marks, gates, dgates, ot, dqt, dm, osend):
    gate = gates[s, t].reshape(64, CH)
    dg = dgates[s, t].reshape(64, CH)
    dc = gate * (dg - jnp.sum(gate * dg, axis=0, keepdims=True))
    dcb = dc.astype(jnp.bfloat16)
    mk = marks[:, :, s * HD:(s + 1) * HD].reshape(64, HD).astype(jnp.bfloat16)
    dq = dqt[s, t] + dot(mk, dcb, TN)
    osend[Q, s, t] = ot[s, t].T.astype(jnp.bfloat16)
    osend[D, s, t] = (dq * SCALE).T.astype(jnp.bfloat16)
    dm[:, :, s * HD:(s + 1) * HD] += (dot(dcb, q[s, rows(t), :], NN) * SCALE).reshape(8, 8, HD)


def remote(src, dst, send, recv, **where):
    return pltpu.make_async_remote_copy(
        src_ref=src, dst_ref=dst, send_sem=send, recv_sem=recv, device_id=where, device_id_type=MESH)


def kernel(nz, nh, k_in, v_in, q_in, d_in, marks_in, sel_in,
           dk_out, dv_out, o_out, dq_out, dm_out,
           xb, k_win, v_win, q_all, d_all, marks_own, sel_own, marks, sel, gsend, gback, osend, dm, dmback, dmsend,
           kt, vt, gates, dgates, ot, dqt, dk, dv,
           x_loc, x_send, x_recv, y_loc, y_send, y_recv, z_send, z_recv,
           s_loc, s_send, s_recv, mz_send, mz_recv, g_send, g_recv, gm_send, gm_recv,
           o_loc, o_send, o_recv):
    z, y, h = lax.axis_index("z"), lax.axis_index("y"), lax.axis_index("head")
    up, down = lax.rem(z + 1, nz), lax.rem(z + nz - 1, nz)
    inputs = (k_in, v_in, q_in, d_in)
    outs = (dk_out, dv_out, o_out, dq_out)
    part = k_in.shape[0]
    half = NY * HD
    wide = HPD * half
    mine = pl.ds(pl.multiple_of(h * part, part), part)

    def to_y(k):
        return lax.rem(y + k, NY)

    def from_y(k):
        return lax.rem(y + NY - k, NY)

    def cols(c, n=HD, base=0):
        return pl.ds(pl.multiple_of(base + c * n, HD), n)

    barrier = pltpu.get_barrier_semaphore()
    for k in range(1, nh):
        pl.semaphore_signal(barrier, inc=1, device_id={"head": lax.rem(h + k, nh)}, device_id_type=MESH)
    for k in range(1, NY):
        pl.semaphore_signal(barrier, inc=1, device_id={"y": to_y(k)}, device_id_type=MESH)
    for other in (up, down):
        pl.semaphore_signal(barrier, inc=1, device_id={"z": other}, device_id_type=MESH)
    pl.semaphore_wait(barrier, nh + NY)

    def x_copies(s, a):
        out = []
        for k in range(1, nh):
            to = lax.rem(h + k, nh)
            out.append(remote(
                inputs[a].at[:, pl.ds(pl.multiple_of(to * wide + s * half, half), half)],
                xb.at[s, a, mine, :], x_send.at[4 * s + a, k], x_recv.at[4 * s + a, k], head=to))
        return out

    def x_local(s, a):
        return pltpu.make_async_copy(
            inputs[a].at[:, pl.ds(pl.multiple_of(h * wide + s * half, half), half)],
            xb.at[s, a, mine, :], x_loc.at[4 * s + a])

    def x_start(s, a):
        for c in x_copies(s, a):
            c.start()
        x_local(s, a).start()

    def x_wait(s, a):
        for c in x_copies(s, a):
            c.wait_recv()
        x_local(s, a).wait()

    def own_rows(s, a, c):
        if a == K:
            return k_win.at[s, rows(NY + c), :]
        if a == V:
            return v_win.at[s, rows(NY + c), :]
        return (q_all if a == Q else d_all).at[s, rows(c), :]

    def y_copy(s, a, k):
        to = to_y(k)
        return remote(xb.at[s, a, :, cols(to)], own_rows(s, a, y),
                      y_send.at[4 * s + a, k], y_recv.at[4 * s + a, k], y=to)

    def y_arrival(s, a, k):
        return remote(xb.at[s, a, :, cols(y)], own_rows(s, a, from_y(k)),
                      y_send.at[4 * s + a, k], y_recv.at[4 * s + a, k], y=to_y(k))

    def y_local(s, a):
        return pltpu.make_async_copy(xb.at[s, a, :, cols(y)], own_rows(s, a, y), y_loc.at[4 * s + a])

    def y_start(s, a):
        for k in range(1, NY):
            y_copy(s, a, k).start()
        y_local(s, a).start()

    def y_wait(s, a):
        for k in range(1, NY):
            y_arrival(s, a, k).wait_recv()
        y_local(s, a).wait()

    def z_copy(s, a, k):
        win = (k_win, v_win)[a]
        c = from_y(k)
        src = xb.at[s, a, :, cols(y)] if k == 0 else win.at[s, rows(NY + c), :]
        return remote(src, win.at[s, rows(c), :], z_send.at[2 * s + a, k], z_recv.at[2 * s + a, k], z=up)

    def z_pass(s, a):
        for k in range(1, NY):
            y_arrival(s, a, k).wait_recv()
            z_copy(s, a, k).start()
        y_local(s, a).wait()

    feat = HPD * HD
    mark_loc = pltpu.make_async_copy(marks_own.at[y], marks.at[NY + y], s_loc.at[0])
    sel_loc = pltpu.make_async_copy(sel_own, sel.at[y], s_loc.at[1])

    def mark_copy(k):
        to = to_y(k)
        return remote(marks_own.at[to], marks.at[NY + y], s_send.at[0, k], s_recv.at[0, k], y=to)

    def mark_arrival(k):
        return remote(marks_own.at[y], marks.at[NY + from_y(k)],
                      s_send.at[0, k], s_recv.at[0, k], y=to_y(k))

    def sel_copy(k):
        return remote(sel_own, sel.at[y], s_send.at[1, k], s_recv.at[1, k], y=to_y(k))

    def sel_arrival(k):
        return remote(sel_own, sel.at[from_y(k)], s_send.at[1, k], s_recv.at[1, k], y=to_y(k))

    mark_up = remote(marks.at[pl.ds(NY, NY)], marks.at[pl.ds(0, NY)], mz_send, mz_recv, z=up)

    args = (q_all, d_all, k_win, v_win, kt, vt, gates, dgates, ot, dqt, dk, dv)
    first = (z - 1) * (NY * CB)

    def transpose_chunk(s, kc):
        kt[s, kc] = k_win[s, rows(kc), :].T
        vt[s, kc] = v_win[s, rows(kc), :].T

    def g_copy(s, a, k):
        c = from_y(k)
        return remote(gsend.at[a, s, c], gback.at[a, s, c], g_send.at[2 * s + a, k], g_recv.at[2 * s + a, k], z=down)

    def prepare(s):
        @pl.loop(0, NY)
        def _(t):
            gate_tile(s, t, first, q_all, marks, sel, gates)

    def chunk(s, k):
        c = from_y(k)
        z_copy(s, K, k).wait_recv()
        z_copy(s, V, k).wait_recv()
        transpose_chunk(s, c)
        transpose_chunk(s, c + NY)
        chunk_cells(s, c, *args)
        gsend[K, s, c] = (dk[s, c] * SCALE).astype(jnp.bfloat16)
        g_copy(s, K, k).start()
        gsend[V, s, c] = dv[s, c].astype(jnp.bfloat16)
        g_copy(s, V, k).start()

    def o_copy(s, a, k):
        to = from_y(k)
        return remote(osend.at[a, s, to], outs[a].at[:, cols(y, HD, s * half)],
                      o_send.at[4 * s + a, k], o_recv.at[4 * s + a, k], y=to)

    def o_arrival(s, a, k):
        return remote(osend.at[a, s, 0], outs[a].at[:, cols(to_y(k), HD, s * half)],
                      o_send.at[4 * s + a, k], o_recv.at[4 * s + a, k], y=to_y(k))

    def o_local(s, a):
        return pltpu.make_async_copy(osend.at[a, s, y], outs[a].at[:, cols(y, HD, s * half)], o_loc.at[4 * s + a])

    def o_start(s, a, k):
        if k == 0:
            o_local(s, a).start()
        else:
            o_copy(s, a, k).start()

    def close(s):
        for k in (1, 2, 3, 0):
            close_tile(s, from_y(k), q_all, marks, gates, dgates, ot, dqt, dm, osend)
            o_start(s, Q, k)
            o_start(s, D, k)

    def finish(s):
        for k in range(NY):
            c = from_y(k)
            g_copy(s, K, k).wait_recv()
            osend[K, s, c] = (dk[s, NY + c] * SCALE + gback[K, s, c].astype(jnp.float32)).astype(jnp.bfloat16)
            o_start(s, K, k)
            g_copy(s, V, k).wait_recv()
            osend[V, s, c] = (dv[s, NY + c] + gback[V, s, c].astype(jnp.float32)).astype(jnp.bfloat16)
            o_start(s, V, k)

    x_start(0, K)
    x_start(0, V)
    x_start(0, Q)
    for to in range(NY):
        for s in range(HPD):
            part_of = marks_in[:, s * half + to * HD:s * half + (to + 1) * HD].astype(jnp.float32)
            marks_own[to, :, s * HD:(s + 1) * HD] = jnp.concatenate([part_of, jnp.zeros((8 - CB, HD), jnp.float32)])
    row = lax.broadcasted_iota(jnp.int32, (CB, CH), 0)
    col = lax.broadcasted_iota(jnp.int32, (CB, CH), 1)
    of_block = (col // BLOCK == row).astype(jnp.bfloat16)
    sel_own[...] = dot(sel_in[...].astype(jnp.float32).astype(jnp.bfloat16), of_block, TN)
    mark_loc.start()
    sel_loc.start()
    for k in range(1, NY):
        mark_copy(k).start()
        sel_copy(k).start()

    ot[...] = jnp.zeros_like(ot)
    dqt[...] = jnp.zeros_like(dqt)
    dk[...] = jnp.zeros_like(dk)
    dv[...] = jnp.zeros_like(dv)
    dgates[...] = jnp.zeros_like(dgates)
    dm[...] = jnp.zeros_like(dm)

    x_wait(0, K)
    y_start(0, K)
    z_copy(0, K, 0).start()
    x_start(0, D)
    x_wait(0, V)
    y_start(0, V)
    z_copy(0, V, 0).start()
    x_start(1, K)
    mark_loc.wait()
    sel_loc.wait()
    for k in range(1, NY):
        mark_arrival(k).wait_recv()
        sel_arrival(k).wait_recv()
    mark_up.start()
    z_pass(0, K)
    x_wait(0, Q)
    y_start(0, Q)
    x_start(1, V)
    z_pass(0, V)
    x_wait(0, D)
    y_start(0, D)
    x_start(1, Q)
    x_wait(1, K)
    y_start(1, K)
    z_copy(1, K, 0).start()
    x_start(1, D)
    y_wait(0, Q)
    mark_up.wait_recv()
    prepare(0)
    x_wait(1, V)
    y_start(1, V)
    z_copy(1, V, 0).start()
    y_wait(0, D)
    chunk(0, 0)
    z_pass(1, K)
    chunk(0, 1)
    z_pass(1, V)
    chunk(0, 2)
    x_wait(1, Q)
    y_start(1, Q)
    chunk(0, 3)
    x_wait(1, D)
    y_start(1, D)
    close(0)
    y_wait(1, Q)
    prepare(1)
    y_wait(1, D)
    for k in range(NY):
        chunk(1, k)
    finish(0)
    close(1)

    dmsend[...] = dm[0:NY]
    dm_back = remote(dmsend, dmback, gm_send, gm_recv, z=down)
    dm_back.start()
    finish(1)
    dm_back.wait_recv()
    dm[NY:] = dm[NY:] + dmback[...]

    def dm_copy(k):
        to = from_y(k)
        return remote(dm.at[NY + to], dm_out.at[:, cols(y, feat)], s_send.at[2, k], s_recv.at[2, k], y=to)

    def dm_arrival(k):
        return remote(dm.at[NY], dm_out.at[:, cols(to_y(k), feat)], s_send.at[2, k], s_recv.at[2, k], y=to_y(k))

    dm_local = pltpu.make_async_copy(dm.at[NY + y], dm_out.at[:, cols(y, feat)], s_loc.at[2])
    for k in range(1, NY):
        dm_copy(k).start()
    dm_local.start()

    for s in range(HPD):
        for a in range(4):
            for c in x_copies(s, a):
                c.wait_send()
            for k in range(1, NY):
                y_copy(s, a, k).wait_send()
                o_copy(s, a, k).wait_send()
                o_arrival(s, a, k).wait_recv()
            o_local(s, a).wait()
        for a in (K, V):
            for k in range(NY):
                z_copy(s, a, k).wait_send()
                g_copy(s, a, k).wait_send()
    for k in range(1, NY):
        mark_copy(k).wait_send()
        sel_copy(k).wait_send()
        dm_copy(k).wait_send()
        dm_arrival(k).wait_recv()
    dm_local.wait()
    mark_up.wait_send()
    dm_back.wait_send()


def hand_over(*refs):
    for n in range(4):
        refs[5 + n][...] = refs[n][...]
    for y in range(NY):
        for s in range(HPD):
            to = (s * NY + y) * HD
            at = (y * HPD + s) * HD
            refs[9][:, to:to + HD] = refs[4][0:CB, at:at + HD].astype(jnp.bfloat16)


def per_device(queries, keys, values, landmarks, grad_out, selections):
    nz, nh = lax.axis_size("z"), lax.axis_size("head")
    width = landmarks.shape[1]
    b, f = jnp.bfloat16, jnp.float32
    hbm, vmem = pl.BlockSpec(memory_space=pl.ANY), pl.BlockSpec(memory_space=pltpu.VMEM)
    big = jax.ShapeDtypeStruct((CH, width), b)
    tall = NY * CH
    feat = HPD * HD
    sem = pltpu.SemaphoreType.DMA
    dk, dv, o, dq, dm = pl.pallas_call(
        lambda *refs: kernel(nz, nh, *refs),
        out_shape=[big] * 4 + [jax.ShapeDtypeStruct((8, width), f)],
        in_specs=[hbm] * 4 + [vmem] * 2,
        out_specs=[hbm] * 4 + [hbm],
        scratch_shapes=[
            pltpu.VMEM((HPD, 4, CH, NY * HD), b),
            pltpu.VMEM((HPD, 2 * tall, HD), b),
            pltpu.VMEM((HPD, 2 * tall, HD), b),
            pltpu.VMEM((HPD, tall, HD), b),
            pltpu.VMEM((HPD, tall, HD), b),
            pltpu.VMEM((NY, 8, feat), f),
            pltpu.VMEM((selections.shape[1], CH), f),
            pltpu.VMEM((8, 8, feat), f),
            pltpu.VMEM((NY, selections.shape[1], CH), f),
            pltpu.VMEM((2, HPD, NY, CH, HD), b),
            pltpu.VMEM((2, HPD, NY, CH, HD), b),
            pltpu.VMEM((4, HPD, NY, CH, HD), b),
            pltpu.VMEM((8, 8, feat), f),
            pltpu.VMEM((NY, 8, feat), f),
            pltpu.VMEM((NY, 8, feat), f),
            pltpu.VMEM((HPD, 8, HD, CH), b),
            pltpu.VMEM((HPD, 8, HD, CH), b),
            pltpu.VMEM((HPD, NY, 8, 8, CH), f),
            pltpu.VMEM((HPD, NY, 8, 8, CH), f),
            pltpu.VMEM((HPD, NY, HD, CH), f),
            pltpu.VMEM((HPD, NY, HD, CH), f),
            pltpu.VMEM((HPD, 8, CH, HD), f),
            pltpu.VMEM((HPD, 8, CH, HD), f),
            sem((8,)), sem((8, 8)), sem((8, 8)),
            sem((8,)), sem((8, 4)), sem((8, 4)),
            sem((4, 4)), sem((4, 4)),
            sem((3,)), sem((3, 4)), sem((3, 4)),
            sem, sem,
            sem((4, 4)), sem((4, 4)), sem, sem,
            sem((8,)), sem((8, 4)), sem((8, 4)),
        ],
        compiler_params=pltpu.CompilerParams(
            collective_id=0, has_side_effects=True, vmem_limit_bytes=63 * 1024 * 1024),
    )(keys, values, queries, grad_out, landmarks, selections)
    piece = pl.BlockSpec((CH // 4, width), lambda n: (n, 0))
    return pl.pallas_call(
        hand_over,
        grid=(4,),
        out_shape=[big] * 4 + [jax.ShapeDtypeStruct((CB, width), b)],
        in_specs=[piece] * 4 + [pl.BlockSpec((8, width), lambda n: (0, 0))],
        out_specs=[piece] * 4 + [pl.BlockSpec((CB, width), lambda n: (0, 0))],
        compiler_params=pltpu.CompilerParams(vmem_limit_bytes=60 * 1024 * 1024),
    )(o, dq, dk, dv, dm)


def solution(mesh):
    shape = (mesh.shape["seq"] // NY, NY, mesh.shape["head"])
    split = jax.sharding.Mesh(mesh.devices.reshape(shape), ("z", "y", "head"))
    rows_all = P(("z", "y", "head"), None)
    out = P(("z", "y"), "head")
    return jax.shard_map(
        per_device, mesh=split,
        in_specs=(rows_all, rows_all, rows_all, out, rows_all, P(("z", "y"), None)),
        out_specs=(out,) * 5, check_vma=False)
```

time: 232 us -> 81.6 us (0.35)
  the two profiles are of different devices: /device:TPU:2 before, /device:TPU:1 now
where the time goes in v3:
time: 81.6 us; the launch traced here: 81.3 us
  Pallas kernels  80.5 us (99%)
    pallas_call x1, Pallas kernels, per_device(): pl.pallas_call(lambda *refs: kernel(nz, nh, *refs), out_shape=[big] * 4 +...  76.7 us
    pallas_call x1, Pallas kernels, per_device(): pl.pallas_call(hand_over, grid=(4,), out_shape=[big] * 4 + [jax.ShapeDtyp...  3.82 us

profile of v3, /device:TPU:1, one launch (start us, length us, event | category | flops | bytes accessed | tf_op | source)
XLA Modules:
  0.0 81.3 jit_solution(14427223704365897297)
XLA Ops:
  0.6 76.7 %shard_map.101 = (bf16[256,1024]{1,0:T(8,128)(2,1)}, bf16[256,1024]{1,0:T(8,128)(2,1)}, bf16[256,1024]{1,0:T(8,128)(2,1)}, bf16[256,1024]{1,0:T(8,128)(2,1)}, f32[8,1024]{1,0:T(8,128)}) custom-call(bf16[32,8192]{1,0:T(8,128)(2,1)} %refs_0_.1, bf16[32,8192]{1,0:T(8,128)(2,1)} %refs_1_.1, bf16[32,8192]{1,0:T(8,128)(2,1)} %refs_2_.1, bf16[32,8192]{1,0:T(8,128)(2,1)} %refs_3_.1, ...), custom_call_target="tpu_custom_call" | custom-call | tf_op jit(solution)/shard_map/pallas_call | solution.py:425
  77.4 3.8 %shard_map.102 = (bf16[256,1024]{1,0:T(8,128)(2,1)}, bf16[256,1024]{1,0:T(8,128)(2,1)}, bf16[256,1024]{1,0:T(8,128)(2,1)}, bf16[256,1024]{1,0:T(8,128)(2,1)}, bf16[4,1024]{1,0:T(4,128)(2,1)}) custom-call(bf16[256,1024]{1,0:T(8,128)(2,1)} %get-tuple-element.10.refs_0_, bf16[256,1024]{1,0:T(8,128)(2,1)} %get-tuple-element.11.refs_1_, ...), custom_call_target="tpu_custom_call" | custom-call | tf_op jit(solution)/shard_map/pallas_call | solution.py:466

commit v4 on v3

--- a/solution.py
+++ b/solution.py
@@ -275,8 +275,8 @@
             o_start(s, Q, k)
             o_start(s, D, k)
 
-    def finish(s):
-        for k in range(NY):
+    def finish(s, turns):
+        for k in turns:
             c = from_y(k)
             g_copy(s, K, k).wait_recv()
             osend[K, s, c] = (dk[s, NY + c] * SCALE + gback[K, s, c].astype(jnp.float32)).astype(jnp.bfloat16)
@@ -355,16 +355,20 @@
     close(0)
     y_wait(1, Q)
     prepare(1)
+    finish(0, (0, 1))
     y_wait(1, D)
-    for k in range(NY):
-        chunk(1, k)
-    finish(0)
+    chunk(1, 0)
+    finish(0, (2,))
+    chunk(1, 1)
+    finish(0, (3,))
+    chunk(1, 2)
+    chunk(1, 3)
     close(1)
 
     dmsend[...] = dm[0:NY]
     dm_back = remote(dmsend, dmback, gm_send, gm_recv, z=down)
     dm_back.start()
-    finish(1)
+    finish(1, range(NY))
     dm_back.wait_recv()
     dm[NY:] = dm[NY:] + dmback[...]
 

time: 81.6 us -> 80.2 us (0.983)
  Pallas kernels: 80.5 us -> 79.2 us
    pallas_call x1, Pallas kernels: 76.7 us -> 75.4 us  [per_device(): pl.pallas_call(lambda *refs: kernel(nz, nh, *refs), out_shape=[big] * 4 +...]
where the time goes in v4:
time: 80.2 us; the launch traced here: 80 us
  Pallas kernels  79.2 us (99%)
    pallas_call x1, Pallas kernels, per_device(): pl.pallas_call(lambda *refs: kernel(nz, nh, *refs), out_shape=[big] * 4 +...  75.4 us
    pallas_call x1, Pallas kernels, per_device(): pl.pallas_call(hand_over, grid=(4,), out_shape=[big] * 4 + [jax.ShapeDtyp...  3.82 us

profile of v4, /device:TPU:1, one launch (start us, length us, event | category | flops | bytes accessed | tf_op | source)
XLA Modules:
  0.0 80.0 jit_solution(4793536748346226650)
XLA Ops:
  0.6 75.4 %shard_map.101 = (bf16[256,1024]{1,0:T(8,128)(2,1)}, bf16[256,1024]{1,0:T(8,128)(2,1)}, bf16[256,1024]{1,0:T(8,128)(2,1)}, bf16[256,1024]{1,0:T(8,128)(2,1)}, f32[8,1024]{1,0:T(8,128)}) custom-call(bf16[32,8192]{1,0:T(8,128)(2,1)} %refs_0_.1, bf16[32,8192]{1,0:T(8,128)(2,1)} %refs_1_.1, bf16[32,8192]{1,0:T(8,128)(2,1)} %refs_2_.1, bf16[32,8192]{1,0:T(8,128)(2,1)} %refs_3_.1, ...), custom_call_target="tpu_custom_call" | custom-call | tf_op jit(solution)/shard_map/pallas_call | solution.py:429
  76.0 3.8 %shard_map.102 = (bf16[256,1024]{1,0:T(8,128)(2,1)}, bf16[256,1024]{1,0:T(8,128)(2,1)}, bf16[256,1024]{1,0:T(8,128)(2,1)}, bf16[256,1024]{1,0:T(8,128)(2,1)}, bf16[4,1024]{1,0:T(4,128)(2,1)}) custom-call(bf16[256,1024]{1,0:T(8,128)(2,1)} %get-tuple-element.10.refs_0_, bf16[256,1024]{1,0:T(8,128)(2,1)} %get-tuple-element.11.refs_1_, ...), custom_call_target="tpu_custom_call" | custom-call | tf_op jit(solution)/shard_map/pallas_call | solution.py:470

commit v5 on v4

--- a/solution.py
+++ b/solution.py
@@ -368,7 +368,7 @@
     dmsend[...] = dm[0:NY]
     dm_back = remote(dmsend, dmback, gm_send, gm_recv, z=down)
     dm_back.start()
-    finish(1, range(NY))
+    finish(1, (0, 1))
     dm_back.wait_recv()
     dm[NY:] = dm[NY:] + dmback[...]
 
@@ -383,6 +383,7 @@
     for k in range(1, NY):
         dm_copy(k).start()
     dm_local.start()
+    finish(1, (2, 3))
 
     for s in range(HPD):
         for a in range(4):

time: 80.2 us -> 80.5 us (level)
  no operation moved by 1% of the time
where the time goes in v5:
time: 80.5 us; the launch traced here: 80.2 us
  Pallas kernels  79.4 us (99%)
    pallas_call x1, Pallas kernels, per_device(): pl.pallas_call(lambda *refs: kernel(nz, nh, *refs), out_shape=[big] * 4 +...  75.6 us
    pallas_call x1, Pallas kernels, per_device(): pl.pallas_call(hand_over, grid=(4,), out_shape=[big] * 4 + [jax.ShapeDtyp...  3.82 us

profile of v5, /device:TPU:1, one launch (start us, length us, event | category | flops | bytes accessed | tf_op | source)
XLA Modules:
  0.0 80.2 jit_solution(10520718296876994986)
XLA Ops:
  0.6 75.6 %shard_map.101 = (bf16[256,1024]{1,0:T(8,128)(2,1)}, bf16[256,1024]{1,0:T(8,128)(2,1)}, bf16[256,1024]{1,0:T(8,128)(2,1)}, bf16[256,1024]{1,0:T(8,128)(2,1)}, f32[8,1024]{1,0:T(8,128)}) custom-call(bf16[32,8192]{1,0:T(8,128)(2,1)} %refs_0_.1, bf16[32,8192]{1,0:T(8,128)(2,1)} %refs_1_.1, bf16[32,8192]{1,0:T(8,128)(2,1)} %refs_2_.1, bf16[32,8192]{1,0:T(8,128)(2,1)} %refs_3_.1, ...), custom_call_target="tpu_custom_call" | custom-call | tf_op jit(solution)/shard_map/pallas_call | solution.py:430
  76.3 3.8 %shard_map.102 = (bf16[256,1024]{1,0:T(8,128)(2,1)}, bf16[256,1024]{1,0:T(8,128)(2,1)}, bf16[256,1024]{1,0:T(8,128)(2,1)}, bf16[256,1024]{1,0:T(8,128)(2,1)}, bf16[4,1024]{1,0:T(4,128)(2,1)}) custom-call(bf16[256,1024]{1,0:T(8,128)(2,1)} %get-tuple-element.10.refs_0_, bf16[256,1024]{1,0:T(8,128)(2,1)} %get-tuple-element.11.refs_1_, ...), custom_call_target="tpu_custom_call" | custom-call | tf_op jit(solution)/shard_map/pallas_call | solution.py:471
